TPU v7x, 256 devices: a whole 4x4x8 slice. The times are simulated.
256 devices in a mesh: blk: 16 (over x, z_hi, core), uly: 16 (over y, z_lo).
Axes of the slice: x: 4, y: 4, z: 8 (z_hi: 2, z_lo: 4; z = z_hi * 4 + z_lo), core: 2. Of those that a mesh axis runs over, the one named last changes fastest.
Arguments:
- queries: bfloat16 [16384, 4096], P(('blk', 'uly')), may hold values from -8 to 8
- gate: bfloat16 [16384, 4096], P(('blk', 'uly')), may hold values from -6 to 6
- keys: bfloat16 [16384, 512], P(('blk', 'uly')), may hold values from -8 to 8
- values: bfloat16 [16384, 512], P(('blk', 'uly')), may hold values from -6 to 6
- q_gain: float32 [256], replicated, may hold values from 0.7 to 5
- k_gain: float32 [256], replicated, may hold values from 0.7 to 5
- span_of: int32 [32], replicated, may hold values from 0 to 31, each once
Outputs:
- gated: bfloat16 [16384, 4096], P(('blk', 'uly'))
Inputs may be any that keep to these rules, and one draw needn't show every extreme that they name: span_of is a permutation of 0 to 31.
All inputs are finite; a program needn't handle non-finite values.
Results may differ from a plain program's by a relative error of at most 0.0085.
The roundings to bfloat16 on the way count: a program that leaves them out, or rounds other values in their place, can miss the bound.
Values may be sent and summed in bfloat16 or wider, within the bound.
No kernel may reach another device: no remote copies, remote signals or barrier semaphores. Data moves between devices by JAX's collectives and lax.ppermute only.
A program may use at most 64 MiB of HBM per device.

v0:
```python
import functools

import jax
import jax.numpy as jnp
from jax import lax
from jax.experimental import pallas as pl
from jax.experimental.pallas import tpu as pltpu
from jax.sharding import PartitionSpec as P

ROTARY = 64
ROPE_BASE = 10000000.0
EPSILON = 1e-06
LOG2E = 1.4426950408889634

GRID = (4, 2, 2, 4, 4)
AXES = ("blk", "uly")
ROWS = 64
DIM = 256
GROUP = 8
TILE = GROUP * ROWS
STATS = 16
SPAN = 512
CHUNK = 128
SHIFTS = (0, 1, 3, 2)

HIDDEN = -1e30
EMPTY = -1e25


def place_of(index):
    place = []
    for extent in reversed(GRID):
        place.append(index % extent)
        index //= extent
    return tuple(reversed(place))


def index_of(place):
    index = 0
    for extent, at in zip(GRID, place):
        index = index * extent + at
    return index


def send(array, target):
    count = index_of(tuple(extent - 1 for extent in GRID)) + 1
    route = [(i, index_of(target(*place_of(i)))) for i in range(count)]
    return lax.ppermute(array, AXES, route)


def to_mate(x, zh, c, y, zl):
    return (x, zh, c, y, zl ^ 1)


def to_far(flip):
    return lambda x, zh, c, y, zl: (x, zh ^ 1, c, y, zl ^ flip)


def along_z(even):
    def target(x, zh, c, y, zl):
        z = (zh * 4 + zl + (-even if zl & 1 else even)) % 8
        return (x, z // 4, c, y, z % 4)

    return target


def to_core(x, zh, c, y, zl):
    return (x, zh, c ^ 1, y, zl)


def to_ring(shift, phase):
    def target(x, zh, c, y, zl):
        if c == phase:
            return ((x + shift) % 4, zh, c, y, zl)
        return (x, zh, c, (y + shift) % 4, zl)

    return target


def whole(*shape):
    return pl.BlockSpec(shape, lambda *_: (0,) * len(shape))


def turned(piece, gain, cosine, sine):
    piece = piece.astype(jnp.float32)
    scale = lax.rsqrt(jnp.mean(piece * piece, axis=-1, keepdims=True) + EPSILON)
    piece = piece * scale * gain
    front = piece[:, :128]
    lane = lax.broadcasted_iota(jnp.int32, front.shape, 1)
    half = ROTARY // 2
    partner = jnp.where(lane < half, pltpu.roll(front, 128 - half, 1), pltpu.roll(front, half, 1))
    front = front * cosine + partner * sine
    return jnp.concatenate([front, piece[:, 128:]], axis=-1).astype(jnp.bfloat16)


def split_kernel(place, keys, values, own, other, done):
    side = place[4] & 1
    copies = []
    for n, (head, out) in enumerate(((side, own), (1 - side, other))):
        columns = pl.ds(pl.multiple_of(head * DIM, DIM), DIM)
        for m, source in enumerate((keys, values)):
            rows = pl.ds(m * ROWS, ROWS)
            copies.append(
                pltpu.make_async_copy(
                    source.at[:, columns], out.at[rows], done.at[2 * n + m]
                )
            )
    for copy in copies:
        copy.start()
    for copy in copies:
        copy.wait()


def ring_source(at, shift):
    return (at + 4 - shift) & 3


def start_kernel(place, span_of, frequency, starts, angles):
    x, zh, c, y, zl = (place[n] for n in range(5))
    side = zl & 1

    def first_position(xs, zhs, cs, ys, within):
        slot = ((xs * 2 + zhs) * 2 + cs) * 2 + (ys >> 1)
        return span_of[slot] * SPAN + (ys & 1) * (SPAN // 2) + within

    z = zh * 4 + zl
    z_next = (z + jnp.where(side == 0, 7, 1)) & 7
    for core in range(2):
        for n, at in enumerate((z, z_next)):
            starts[2 * core + n] = first_position(
                x, at >> 2, c ^ core, y, ((at & 3) >> 1) * CHUNK
            )
    for a, outer in enumerate(SHIFTS):
        for b, inner in enumerate(SHIFTS):
            xs = jnp.where(c == 0, ring_source(x, inner), ring_source(x, outer))
            ys = jnp.where(c == 0, ring_source(y, outer), ring_source(y, inner))
            for t in range(2):
                starts[4 + a * 8 + b * 2 + t] = first_position(
                    xs, zh ^ t, c, ys, (zl >> 1) * CHUNK
                )
    row = lax.broadcasted_iota(jnp.int32, (ROWS, 128), 0)
    firsts = [starts[0] + side * ROWS]
    firsts += [starts[4 + t] + (side ^ n) * ROWS for t in range(2) for n in range(2)]
    for n, first in enumerate(firsts):
        angles[n * ROWS : (n + 1) * ROWS] = (row + first).astype(jnp.float32) * frequency[...]


STAGES = ((0, 8), (8, 16), (24, 8))
PER_TILE = 72
NEVER = -(1 << 20)


def plan_kernel(place, starts, q_gain, k_gain, plan):
    for tile in range(4):
        base = tile * PER_TILE

        def clear(n, carry):
            plan[base + n] = 0
            plan[base + 32 + n] = NEVER
            return carry

        lax.fori_loop(0, 32, clear, 0)
        for stage, (first, chunks) in enumerate(STAGES):

            def visit(j, count):
                reach = starts[tile] - starts[4 + first + j]
                seen = reach > -CHUNK
                at = base + first + count

                @pl.when(seen)
                def _():
                    plan[at] = j
                    plan[at + 32] = reach

                return count + seen.astype(jnp.int32)

            count = lax.fori_loop(0, chunks, visit, jnp.int32(0))
            plan[base + 64 + stage] = (count + 3) >> 2
    plan[4 * PER_TILE] = place[4] & 1
    bound = jnp.max(jnp.abs(q_gain[...])) * jnp.max(jnp.abs(k_gain[...])) * (16.0 * 1.02 * LOG2E)
    plan[4 * PER_TILE + 1] = (bound <= 100.0).astype(jnp.int32)


def keys_kernel(own, mate, far, cross, gain, cosine, sine, out):
    for n, piece in enumerate((own, mate, far, cross)):
        at = slice(n * ROWS, (n + 1) * ROWS)
        t, low = n // 2, (n % 2) * ROWS
        out[t, low : low + ROWS] = turned(piece[:ROWS], gain[...], cosine[at], sine[at])
        out[t, CHUNK + low : CHUNK + low + ROWS] = piece[ROWS:]


def queries_kernel(place, queries, gain, cosine, sine, own, other):
    side = place[4] & 1
    for head, out in ((side, own), (1 - side, other)):
        for member in range(GROUP):
            columns = pl.ds(pl.multiple_of((head * GROUP + member) * DIM, DIM), DIM)
            piece = turned(queries[:, columns], gain[...], cosine[...], sine[...])
            out[member * ROWS : (member + 1) * ROWS] = piece * jnp.bfloat16(DIM**-0.5)


def attend_kernel(stage, first_tile, buffers, plan, queries, *refs):
    first, last = stage == 0, stage == 2
    stores, refs = refs[:buffers], list(refs[buffers:])
    if not first:
        del refs[:3]
    if last:
        out = refs.pop(0)
    top, total, acc = refs
    side = plan[4 * PER_TILE]
    bounded = plan[4 * PER_TILE + 1] == 1
    per_store = stores[0].shape[0]

    if first:
        top[...] = jnp.full(top.shape, jnp.where(bounded, 0.0, EMPTY), jnp.float32)
        total[...] = jnp.zeros(total.shape, jnp.float32)
        acc[...] = jnp.zeros(acc.shape, jnp.float32)

    def fetch(j, part):
        rows = slice(part * CHUNK, (part + 1) * CHUNK)
        if buffers == 1:
            return stores[0][j, rows]
        within = lax.rem(j, per_store)
        return jnp.where(j >= per_store, stores[1][within, rows], stores[0][within, rows])

    row = lax.broadcasted_iota(jnp.int32, (TILE, CHUNK), 0)
    lane = lax.broadcasted_iota(jnp.int32, (TILE, CHUNK), 1)

    def gather(tile, n):
        at = (first_tile + tile) * PER_TILE + STAGES[stage][0] + 4 * n
        picks = [plan[at + m] for m in range(4)]
        limits = [plan[at + 32 + m] for m in range(4)]
        keys = jnp.concatenate([fetch(j, 0) for j in picks], axis=0)
        values = jnp.concatenate([fetch(j, 1) for j in picks], axis=0)
        return keys, values, limits

    def scores_of(tile, piece, rows, keys, limits):
        scores = lax.dot_general(
            queries[tile, rows],
            keys,
            (((1,), (1,)), ((), ())),
            preferred_element_type=jnp.float32,
        )
        scores = scores * LOG2E
        gap = (lane ^ (side * ROWS)) - (row & (ROWS - 1)) - (side ^ piece) * ROWS
        return [
            jnp.where(gap <= limit, scores[:, m * CHUNK : (m + 1) * CHUNK], HIDDEN)
            for m, limit in enumerate(limits)
        ]

    def add(tile, rows, parts, values):
        weights = [jnp.exp2(part) for part in parts]
        total[tile, rows] += functools.reduce(jnp.add, weights)
        acc[tile, rows] += jnp.dot(
            jnp.concatenate(weights, axis=-1).astype(jnp.bfloat16),
            values,
            preferred_element_type=jnp.float32,
        )

    bases = [(first_tile + tile) * PER_TILE for tile in range(2)]
    steps = jnp.maximum(plan[bases[0] + 64 + stage], plan[bases[1] + 64 + stage])

    @pl.when(bounded)
    def _():
        def step(n, carry):
            for tile in range(2):
                keys, values, limits = gather(tile, n)
                for piece in range(2):
                    rows = slice(piece * TILE, (piece + 1) * TILE)
                    add(tile, rows, scores_of(tile, piece, rows, keys, limits), values)
            return carry

        lax.fori_loop(0, steps, step, 0)

    @pl.when(jnp.logical_not(bounded))
    def _():
        def step(n, carry):
            tile, piece = (n >> 1) & 1, n & 1
            keys, values, limits = gather(tile, n >> 2)
            rows = pl.ds(pl.multiple_of(piece * TILE, TILE), TILE)
            parts = scores_of(tile, piece, rows, keys, limits)
            before = top[tile, rows]
            peak = functools.reduce(jnp.maximum, parts)
            now = jnp.maximum(before, jnp.max(peak, axis=-1, keepdims=True))
            fading = jnp.exp2(before - now)
            top[tile, rows] = now
            total[tile, rows] = total[tile, rows] * fading
            acc[tile, rows] = acc[tile, rows] * jnp.concatenate([fading, fading], axis=-1)
            add(tile, rows, [part - now for part in parts], values)
            return carry

        lax.fori_loop(0, 4 * steps, step, 0)

    if last:
        for tile in range(2):
            for piece in range(2):
                logs = []
                for sub in range(TILE // 128):
                    rows = slice(piece * TILE + sub * 128, piece * TILE + (sub + 1) * 128)
                    sums = jnp.sum(total[tile, rows], axis=-1, keepdims=True)
                    some = sums > 0.0
                    sums = jnp.where(some, sums, 1.0)
                    result = (acc[tile, rows] / sums).astype(jnp.bfloat16)
                    out[2 * tile + piece, sub * 128 : (sub + 1) * 128] = result
                    level = jnp.where(some, top[tile, rows] + jnp.log2(sums), EMPTY)
                    logs.append(level.T[:1])
                out[2 * tile + piece, TILE:] = packed(logs)


def packed(logs):
    level = jnp.concatenate(logs, axis=0)
    high = level.astype(jnp.bfloat16).astype(jnp.float32)
    middle = (level - high).astype(jnp.bfloat16).astype(jnp.float32)
    low = level - high - middle
    rows = jnp.concatenate([high, middle, low, jnp.zeros_like(low)], axis=0)
    return jnp.concatenate([rows, jnp.zeros_like(rows)], axis=-1).astype(jnp.bfloat16)


def unpacked(rows):
    rows = rows[:, :128].astype(jnp.float32)
    return rows[0:4] + rows[4:8] + rows[8:12]


def blend(left, right):
    a, b = unpacked(left), unpacked(right)
    peak = jnp.maximum(a, b)
    a, b = jnp.exp2(a - peak), jnp.exp2(b - peak)
    both = a + b
    return a / both, b / both, peak + jnp.log2(both)


def column(shares, n):
    share = jnp.broadcast_to(shares[n : n + 1], (128, 128)).T
    return jnp.concatenate([share, share], axis=-1)


def join_kernel(mine, theirs, *outs):
    for r, out in enumerate(outs):
        a, b, level = blend(mine[r, TILE:], theirs[r, TILE:])
        for n in range(TILE // 128):
            rows = slice(n * 128, (n + 1) * 128)
            left = mine[r, rows].astype(jnp.float32) * column(a, n)
            right = theirs[r, rows].astype(jnp.float32) * column(b, n)
            out[rows] = (left + right).astype(jnp.bfloat16)
        out[TILE:] = packed([level])


def finish_kernel(place, near0, near1, far0, far1, gate, out):
    side = place[4] & 1
    for which, (left_ref, right_ref) in enumerate(((near0, far0), (near1, far1))):
        head = side if which == 0 else 1 - side
        a, b, _ = blend(left_ref[TILE:], right_ref[TILE:])
        for n in range(TILE // 128):
            rows = slice(n * 128, (n + 1) * 128)
            left = left_ref[rows].astype(jnp.float32) * column(a, n)
            right = right_ref[rows].astype(jnp.float32) * column(b, n)
            attended = (left + right).astype(jnp.bfloat16).astype(jnp.float32)
            for m in range(2):
                at = (head * GROUP + 2 * n + m) * DIM
                columns = pl.ds(pl.multiple_of(at, DIM), DIM)
                logits = gate[:, columns].astype(jnp.float32)
                gated = attended[m * ROWS : (m + 1) * ROWS] * jax.nn.sigmoid(logits)
                out[:, columns] = gated.astype(jnp.bfloat16)


SMEM = pl.BlockSpec(memory_space=pltpu.SMEM)
VMEM = pl.BlockSpec(memory_space=pltpu.VMEM)
BIG = pltpu.CompilerParams(vmem_limit_bytes=28 * 1024 * 1024)


def attend(plan, queries, stores, state, stage, first_tile):
    shapes = [
        jax.ShapeDtypeStruct((2, 2 * TILE, width), jnp.float32) for width in (128, 128, DIM)
    ]
    if stage == 2:
        shapes = [jax.ShapeDtypeStruct((4, TILE + STATS, DIM), jnp.bfloat16)] + shapes
    given = 2 + len(stores)
    aliases = {given + n: n + (stage == 2) for n in range(len(state))}
    chunks = STAGES[stage][1]
    return pl.pallas_call(
        functools.partial(attend_kernel, stage, first_tile, len(stores)),
        in_specs=[SMEM] + [VMEM] * (1 + len(stores) + len(state)),
        out_specs=[VMEM] * len(shapes),
        out_shape=shapes,
        input_output_aliases=aliases,
        compiler_params=BIG,
        cost_estimate=pl.CostEstimate(
            flops=4 * 4 * TILE * chunks * CHUNK * DIM,
            bytes_accessed=4 << 20,
            transcendentals=4 * TILE * chunks * CHUNK,
        ),
    )(plan, queries, *stores, *state)


def local(queries, gate, keys, values, q_gain, k_gain, span_of):
    index = lax.axis_index("blk") * 16 + lax.axis_index("uly")
    place = jnp.stack(place_of(index)).astype(jnp.int32)
    q_gain, k_gain = q_gain.reshape(1, DIM), k_gain.reshape(1, DIM)

    pair = jax.ShapeDtypeStruct((2 * ROWS, DIM), jnp.bfloat16)
    kv_own, kv_other = pl.pallas_call(
        split_kernel,
        in_specs=[SMEM] + [pl.BlockSpec(memory_space=pl.ANY)] * 2,
        out_specs=[VMEM] * 2,
        out_shape=[pair, pair],
        scratch_shapes=[pltpu.SemaphoreType.DMA((4,))],
        compiler_params=BIG,
    )(place, keys, values)
    far = send(kv_own, to_far(0))
    cross = send(kv_other, to_far(1))
    mate = send(kv_other, to_mate)
    span_of, _ = lax.optimization_barrier((span_of, kv_own))

    lane = jnp.arange(128, dtype=jnp.int32)
    frequency = ROPE_BASE ** (-2.0 * (lane % 32).astype(jnp.float32) / ROTARY)
    starts, angles = pl.pallas_call(
        start_kernel,
        in_specs=[SMEM] * 2 + [VMEM],
        out_specs=[SMEM, VMEM],
        out_shape=[
            jax.ShapeDtypeStruct((36,), jnp.int32),
            jax.ShapeDtypeStruct((5 * ROWS, 128), jnp.float32),
        ],
        compiler_params=BIG,
    )(place, span_of, frequency.reshape(1, 128))
    rotated = lane[None, :] < ROTARY
    cosine = jnp.where(rotated, jnp.cos(angles), 1.0)
    sine = jnp.sin(angles)
    sine = jnp.where(rotated, jnp.where(lane[None, :] < ROTARY // 2, -sine, sine), 0.0)

    tile = jax.ShapeDtypeStruct((TILE, DIM), jnp.bfloat16)
    q_own, q_other = pl.pallas_call(
        queries_kernel,
        in_specs=[SMEM] + [VMEM] * 4,
        out_specs=[VMEM] * 2,
        out_shape=[tile, tile],
        compiler_params=BIG,
    )(place, queries, q_gain, cosine[:ROWS], sine[:ROWS])
    mate, far, cross, q_own, q_other = lax.optimization_barrier((mate, far, cross, q_own, q_other))

    base = pl.pallas_call(
        keys_kernel,
        in_specs=[VMEM] * 7,
        out_specs=VMEM,
        out_shape=jax.ShapeDtypeStruct((2, 2 * CHUNK, DIM), jnp.bfloat16),
        compiler_params=BIG,
    )(kv_own, mate, far, cross, k_gain, cosine[ROWS:], sine[ROWS:])

    plan = pl.pallas_call(
        plan_kernel,
        in_specs=[SMEM] * 2 + [VMEM] * 2,
        out_specs=SMEM,
        out_shape=jax.ShapeDtypeStruct((4 * PER_TILE + 8,), jnp.int32),
        compiler_params=BIG,
    )(place, starts, q_gain, k_gain)

    store = [base] + [send(base, to_ring(s, 0)) for s in SHIFTS[1:]]
    store = jnp.concatenate(store, axis=0)
    q_mine = jnp.stack(
        [q_own, send(q_other, to_mate), send(q_own, along_z(2)), send(q_other, along_z(-1))]
    ).reshape(2, 2 * TILE, DIM)
    store, q_mine, plan = lax.optimization_barrier((store, q_mine, plan))
    q_theirs = send(q_mine, to_core)
    arrived = [send(store, to_ring(s, 1)) for s in SHIFTS[1:3]]
    mine = attend(plan, q_mine, [store], [], 0, 0)
    theirs = attend(plan, q_theirs, [store], [], 0, 2)

    arrived, mine, theirs = lax.optimization_barrier((arrived, mine, theirs))
    last = [
        send(arrived[0][:4], to_ring(1, 1)),
        send(arrived[1][4:], to_ring(3, 1)),
    ]
    mine = attend(plan, q_mine, arrived, mine, 1, 0)
    theirs = attend(plan, q_theirs, arrived, theirs, 1, 2)
    last, mine, theirs = lax.optimization_barrier((last, mine, theirs))
    out_theirs = attend(plan, q_theirs, last, theirs, 2, 2)[0]
    received = send(out_theirs, to_core)
    out_mine = attend(plan, q_mine, last, mine, 2, 0)[0]

    joint = jax.ShapeDtypeStruct((TILE + STATS, DIM), jnp.bfloat16)
    parts = pl.pallas_call(
        join_kernel,
        in_specs=[VMEM] * 2,
        out_specs=[VMEM] * 4,
        out_shape=[joint] * 4,
        compiler_params=BIG,
    )(out_mine, received)
    home = [
        parts[0],
        send(parts[1], to_mate),
        send(parts[2], along_z(-2)),
        send(parts[3], along_z(-1)),
    ]

    return pl.pallas_call(
        finish_kernel,
        in_specs=[SMEM] + [VMEM] * 5,
        out_specs=VMEM,
        out_shape=jax.ShapeDtypeStruct(queries.shape, jnp.bfloat16),
        compiler_params=BIG,
    )(place, *home, gate)


def solution(mesh):
    rows = P(("blk", "uly"), None)
    in_specs = (rows, rows, rows, rows, P(), P(), P())
    return jax.shard_map(local, mesh=mesh, in_specs=in_specs, out_specs=rows, check_vma=False)
```

profile of v0, /device:TPU:6, one launch (start us, length us, event | category | flops | bytes accessed | tf_op | source)
XLA Modules:
  0.0 122.9 jit_solution(7384518952658795266)
XLA Ops:
  2.4 6.8 %collective-permute-start.2 = (bf16[128,256]{1,0:T(8,128)(2,1)S(1)}, bf16[128,256]{1,0:T(8,128)(2,1)S(1)}, u32[]{:S(2)}, u32[]{:S(2)}) collective-permute-start(bf16[128,256]{1,0:T(8,128)(2,1)S(1)} %get-tuple-element.55), channel_id=1, source_target_pairs={{0,33},{1,32},{2,35},{3,34},{4,37},{5,36},{6,39},{7,38},{8,41},{9,... | collective-permute-start | bytes 196616 | tf_op jit(solution)/shard_map/ppermute | solution.py:48
  11.5 1.3 %shard_map.74 = (s32[36]{0:T(128)S(1)}, f32[320,128]{1,0:T(8,128)S(1)}) custom-call(s32[5]{0:T(128)S(1)} %stack.38.place, s32[32]{0:T(128)S(1)} %copy-done.7, f32[1,128]{1,0:T(1,128)S(1)} %fusion.3.frequency), custom_call_target="tpu_custom_call" | custom-call | tf_op jit(solution)/shard_map/pallas_call | solution.py:415
  13.4 1.0 copy-done.1
  15.1 2.3 %shard_map.75 = (bf16[512,256]{1,0:T(8,128)(2,1)S(1)}, bf16[512,256]{1,0:T(8,128)(2,1)S(1)}) custom-call(s32[5]{0:T(128)S(1)} %stack.38.place, bf16[64,4096]{1,0:T(8,128)(2,1)S(1)} %copy-done.1, f32[1,256]{1,0:T(1,128)S(1)} %bitcast.17, f32[64,128]{1,0:T(8,128)S(1)} %slice.24.cosine, f32[64,128]{1,0:T(8,128)S(1)} %slice.25.sine), custom_call_target="tpu_custom_call" | custom-call | tf_op jit(solution)/shard_map/pallas_call | solution.py:431
  17.4 1.2 collective-permute-done.1.far
  18.6 1.4 %collective-permute-start.7 = (bf16[512,256]{1,0:T(8,128)(2,1)S(1)}, bf16[512,256]{1,0:T(8,128)(2,1)S(1)}, u32[]{:S(2)}, u32[]{:S(2)}) collective-permute-start(bf16[512,256]{1,0:T(8,128)(2,1)S(1)} %get-tuple-element.63), channel_id=1, source_target_pairs={{0,2},{1,35},{2,32},{3,1},{4,6},{5,39},{6,36},{7,5},{8,10},{9,43},... | collective-permute-start | bytes 786440 | tf_op jit(solution)/shard_map/ppermute | solution.py:48
  20.0 3.0 %collective-permute-start.8 = (bf16[512,256]{1,0:T(8,128)(2,1)S(1)}, bf16[512,256]{1,0:T(8,128)(2,1)S(1)}, u32[]{:S(2)}, u32[]{:S(2)}) collective-permute-start(bf16[512,256]{1,0:T(8,128)(2,1)S(1)} %get-tuple-element.64), channel_id=1, source_target_pairs={{0,35},{1,2},{2,1},{3,32},{4,39},{5,6},{6,5},{7,36},{8,43},{9,10},... | collective-permute-start | bytes 786440 | tf_op jit(solution)/shard_map/ppermute | solution.py:48
  23.0 1.0 collective-permute-start.6
  24.4 1.5 %collective-permute-start.5 = (bf16[2,256,256]{2,1,0:T(8,128)(2,1)S(1)}, bf16[2,256,256]{2,1,0:T(8,128)(2,1)S(1)}, u32[]{:S(2)}, u32[]{:S(2)}) collective-permute-start(bf16[2,256,256]{2,1,0:T(8,128)(2,1)S(1)} %shard_map.76), channel_id=1, source_target_pairs={{0,128},{1,129},{2,130},{3,131},{4,132},{5,133},{6,134},{7,135},{8... | collective-permute-start | bytes 786440 | tf_op jit(solution)/shard_map/ppermute | solution.py:48
  25.9 4.1 %collective-permute-done.7 = bf16[512,256]{1,0:T(8,128)(2,1)S(1)} collective-permute-done((bf16[512,256]{1,0:T(8,128)(2,1)S(1)}, bf16[512,256]{1,0:T(8,128)(2,1)S(1)}, u32[]{:S(2)}, u32[]{:S(2)}) %collective-permute-start.7) | collective-permute-done | bytes 262176 | tf_op jit(solution)/shard_map/ppermute | solution.py:48
  30.5 3.5 %shard_map.77.plan = s32[296]{0:T(512)S(1)} custom-call(s32[5]{0:T(128)S(1)} %stack.38.place, s32[36]{0:T(128)S(1)} %get-tuple-element.65.starts, f32[1,256]{1,0:T(1,128)S(1)} %bitcast.18, f32[1,256]{1,0:T(1,128)S(1)} %bitcast.20), custom_call_target="tpu_custom_call" | custom-call | tf_op jit(solution)/shard_map/pallas_call | solution.py:448
  35.2 1.2 collective-permute-done.3
  36.6 3.1 %collective-permute-start.10 = (bf16[8,256,256]{2,1,0:T(8,128)(2,1)S(1)}, bf16[8,256,256]{2,1,0:T(8,128)(2,1)S(1)}, u32[]{:S(2)}, u32[]{:S(2)}) collective-permute-start(bf16[8,256,256]{2,1,0:T(8,128)(2,1)S(1)} %pad_maximum_fusion.refs_0_), channel_id=1, source_target_pairs={{0,12},{1,13},{2,14},{3,15},{4,0},{5,1},{6,2},{7,3},{8,4},{9,5},{1... | collective-permute-start | bytes 3145736 | tf_op jit(solution)/shard_map/ppermute | solution.py:48
  39.7 8.2 %shard_map.78 = (f32[2,1024,128]{2,1,0:T(8,128)S(1)}, f32[2,1024,128]{2,1,0:T(8,128)S(1)}, f32[2,1024,256]{2,1,0:T(8,128)S(1)}) custom-call(s32[296]{0:T(512)S(1)} %shard_map.77.plan, bf16[2,1024,256]{2,1,0:T(8,128)(2,1)S(1)} %bitcast.13, bf16[8,256,256]{2,1,0:T(8,128)(2,1)S(1)} %pad_maximum_fusion.refs_0_), custom_call_target="tpu_custom_call" | custom-call | flops 2147483648 | bytes 4194304 | tf_op jit(solution)/shard_map/pallas_call | solution.py:379
  48.0 8.0 %shard_map.79 = (f32[2,1024,128]{2,1,0:T(8,128)S(1)}, f32[2,1024,128]{2,1,0:T(8,128)S(1)}, f32[2,1024,256]{2,1,0:T(8,128)S(1)}) custom-call(s32[296]{0:T(512)S(1)} %shard_map.77.plan, bf16[2,1024,256]{2,1,0:T(8,128)(2,1)S(1)} %collective-permute-done.11.queries, bf16[8,256,256]{2,1,0:T(8,128)(2,1)S(1)} %pad_maximum_fusion.refs_0_), custom_call_target="tpu_custom_call" | custom-call | flops 2147483648 | bytes 4194304 | tf_op jit(solution)/shard_map/pallas_call | solution.py:379
  56.7 2.7 %collective-permute-start.13 = (bf16[4,256,256]{2,1,0:T(8,128)(2,1)S(1)}, bf16[4,256,256]{2,1,0:T(8,128)(2,1)S(1)}, u32[]{:S(2)}, u32[]{:S(2)}) collective-permute-start(bf16[4,256,256]{2,1,0:T(8,128)(2,1)S(1)} %slice.23), channel_id=1, source_target_pairs={{0,12},{1,13},{2,14},{3,15},{4,0},{5,1},{6,2},{7,3},{8,4},{9,5},{1... | collective-permute-start | bytes 1572872 | tf_op jit(solution)/shard_map/ppermute | solution.py:48
  59.4 15.1 %shard_map.80 = (f32[2,1024,128]{2,1,0:T(8,128)S(1)}, f32[2,1024,128]{2,1,0:T(8,128)S(1)}, f32[2,1024,256]{2,1,0:T(8,128)S(1)}) custom-call(s32[296]{0:T(512)S(1)} %shard_map.77.plan, bf16[2,1024,256]{2,1,0:T(8,128)(2,1)S(1)} %bitcast.14, ...), custom_call_target="tpu_custom_call", output_to_operand_aliasing={{0}: (4, {}), {1}: (5, {}), {2}: (6, {})} | custom-call | flops 4294967296 | bytes 4194304 | tf_op jit(solution)/shard_map/pallas_call | solution.py:379
  74.5 11.4 %shard_map.81 = (f32[2,1024,128]{2,1,0:T(8,128)S(1)}, f32[2,1024,128]{2,1,0:T(8,128)S(1)}, f32[2,1024,256]{2,1,0:T(8,128)S(1)}) custom-call(s32[296]{0:T(512)S(1)} %shard_map.77.plan, bf16[2,1024,256]{2,1,0:T(8,128)(2,1)S(1)} %collective-permute-done.11.queries, ...), custom_call_target="tpu_custom_call", output_to_operand_aliasing={{0}: (4, {}), {1}: (5, {}), {2}: (6, {})} | custom-call | flops 4294967296 | bytes 4194304 | tf_op jit(solution)/shard_map/pallas_call | solution.py:379
  85.9 8.5 %shard_map.83 = (bf16[4,528,256]{2,1,0:T(8,128)(2,1)S(1)}, f32[2,1024,128]{2,1,0:T(8,128)S(1)}, f32[2,1024,128]{2,1,0:T(8,128)S(1)}, f32[2,1024,256]{2,1,0:T(8,128)S(1)}) custom-call(s32[296]{0:T(512)S(1)} %shard_map.77.plan, bf16[2,1024,256]{2,1,0:T(8,128)(2,1)S(1)} %collective-permute-done.11.queries, ...), custom_call_target="tpu_custom_call", output_to_operand_aliasing={{1}: (4, {}), {2}: (5, {}), {3}: (6, {})} | custom-call | flops 2147483648 | bytes 4194304 | tf_op jit(solution)/shard_map/pallas_call | solution.py:379
  94.5 8.7 %shard_map.82 = (bf16[4,528,256]{2,1,0:T(8,128)(2,1)S(1)}, f32[2,1024,128]{2,1,0:T(8,128)S(1)}, f32[2,1024,128]{2,1,0:T(8,128)S(1)}, f32[2,1024,256]{2,1,0:T(8,128)S(1)}) custom-call(s32[296]{0:T(512)S(1)} %shard_map.77.plan, bf16[2,1024,256]{2,1,0:T(8,128)(2,1)S(1)} %bitcast.15, ...), custom_call_target="tpu_custom_call", output_to_operand_aliasing={{1}: (4, {}), {2}: (5, {}), {3}: (6, {})} | custom-call | flops 2147483648 | bytes 4194304 | tf_op jit(solution)/shard_map/pallas_call | solution.py:379
  104.0 4.4 %collective-permute-start.16 = (bf16[528,256]{1,0:T(8,128)(2,1)S(1)}, bf16[528,256]{1,0:T(8,128)(2,1)S(1)}, u32[]{:S(2)}, u32[]{:S(2)}) collective-permute-start(bf16[528,256]{1,0:T(8,128)(2,1)S(1)} %get-tuple-element.101), channel_id=1, source_target_pairs={{0,34},{1,3},{2,0},{3,33},{4,38},{5,7},{6,4},{7,37},{8,42},{9,11},... | collective-permute-start | bytes 811016 | tf_op jit(solution)/shard_map/ppermute | solution.py:48
  108.7 10.0 %collective-permute-done.15.near1 = bf16[528,256]{1,0:T(8,128)(2,1)S(1)} collective-permute-done((bf16[528,256]{1,0:T(8,128)(2,1)S(1)}, bf16[528,256]{1,0:T(8,128)(2,1)S(1)}, u32[]{:S(2)}, u32[]{:S(2)}) %collective-permute-start.15) | collective-permute-done | bytes 270368 | tf_op jit(solution)/shard_map/ppermute | solution.py:48
  118.7 2.4 %collective-permute-done.17.far1 = bf16[528,256]{1,0:T(8,128)(2,1)S(1)} collective-permute-done((bf16[528,256]{1,0:T(8,128)(2,1)S(1)}, bf16[528,256]{1,0:T(8,128)(2,1)S(1)}, u32[]{:S(2)}, u32[]{:S(2)}) %collective-permute-start.17) | collective-permute-done | bytes 270368 | tf_op jit(solution)/shard_map/ppermute | solution.py:48
  121.1 1.8 %shard_map.85 = bf16[64,4096]{1,0:T(8,128)(2,1)} custom-call(s32[5]{0:T(128)S(1)} %stack.38.place, bf16[528,256]{1,0:T(8,128)(2,1)S(1)} %get-tuple-element.99.near0, bf16[528,256]{1,0:T(8,128)(2,1)S(1)} %collective-permute-done.15.near1, bf16[528,256]{1,0:T(8,128)(2,1)S(1)} %collective-permute-done.16.far0, ...), custom_call_target="tpu_custom_call" | custom-call | tf_op jit(solution)/shard_map/pallas_call | solution.py:494
  (53 shorter events, 9.9 us)
Async XLA Ops:
  0.0 30.5 %copy-start.5 = (f32[256]{0:T(256)S(1)}, f32[256]{0:T(256)}, u32[]{:S(2)}) copy-start(f32[256]{0:T(256)} %param.11) | copy-start | bytes 3076
  0.0 24.1 %copy-start.6 = (f32[256]{0:T(256)S(1)}, f32[256]{0:T(256)}, u32[]{:S(2)}) copy-start(f32[256]{0:T(256)} %param.12) | copy-start | bytes 3076
  0.1 0.8 copy-start.2
  0.9 0.8 copy-start.3
  2.4 15.0 %collective-permute-start.2 = (bf16[128,256]{1,0:T(8,128)(2,1)S(1)}, bf16[128,256]{1,0:T(8,128)(2,1)S(1)}, u32[]{:S(2)}, u32[]{:S(2)}) collective-permute-start(bf16[128,256]{1,0:T(8,128)(2,1)S(1)} %get-tuple-element.55), channel_id=1, source_target_pairs={{0,33},{1,32},{2,35},{3,34},{4,37},{5,36},{6,39},{7,38},{8,41},{9,... | collective-permute-start | bytes 196616 | tf_op jit(solution)/shard_map/ppermute | solution.py:48
  9.2 8.2 %collective-permute-start = (bf16[128,256]{1,0:T(8,128)(2,1)S(1)}, bf16[128,256]{1,0:T(8,128)(2,1)S(1)}, u32[]{:S(2)}, u32[]{:S(2)}) collective-permute-start(bf16[128,256]{1,0:T(8,128)(2,1)S(1)} %get-tuple-element.55), channel_id=1, source_target_pairs={{0,1},{1,0},{2,3},{3,2},{4,5},{5,4},{6,7},{7,6},{8,9},{9,8},{10,11... | collective-permute-start | bytes 196616 | tf_op jit(solution)/shard_map/ppermute | solution.py:48
  10.2 8.4 %collective-permute-start.1 = (bf16[128,256]{1,0:T(8,128)(2,1)S(1)}, bf16[128,256]{1,0:T(8,128)(2,1)S(1)}, u32[]{:S(2)}, u32[]{:S(2)}) collective-permute-start(bf16[128,256]{1,0:T(8,128)(2,1)S(1)} %get-tuple-element.54.own), channel_id=1, source_target_pairs={{0,32},{1,33},{2,34},{3,35},{4,36},{5,37},{6,38},{7,39},{8,40},{9,... | collective-permute-start | bytes 196616 | tf_op jit(solution)/shard_map/ppermute | solution.py:48
  13.4 1.0 copy-start.1
  18.6 11.4 %collective-permute-start.7 = (bf16[512,256]{1,0:T(8,128)(2,1)S(1)}, bf16[512,256]{1,0:T(8,128)(2,1)S(1)}, u32[]{:S(2)}, u32[]{:S(2)}) collective-permute-start(bf16[512,256]{1,0:T(8,128)(2,1)S(1)} %get-tuple-element.63), channel_id=1, source_target_pairs={{0,2},{1,35},{2,32},{3,1},{4,6},{5,39},{6,36},{7,5},{8,10},{9,43},... | collective-permute-start | bytes 786440 | tf_op jit(solution)/shard_map/ppermute | solution.py:48
  20.0 14.0 %collective-permute-start.8 = (bf16[512,256]{1,0:T(8,128)(2,1)S(1)}, bf16[512,256]{1,0:T(8,128)(2,1)S(1)}, u32[]{:S(2)}, u32[]{:S(2)}) collective-permute-start(bf16[512,256]{1,0:T(8,128)(2,1)S(1)} %get-tuple-element.64), channel_id=1, source_target_pairs={{0,35},{1,2},{2,1},{3,32},{4,39},{5,6},{6,5},{7,36},{8,43},{9,10},... | collective-permute-start | bytes 786440 | tf_op jit(solution)/shard_map/ppermute | solution.py:48
  23.0 11.0 %collective-permute-start.6 = (bf16[512,256]{1,0:T(8,128)(2,1)S(1)}, bf16[512,256]{1,0:T(8,128)(2,1)S(1)}, u32[]{:S(2)}, u32[]{:S(2)}) collective-permute-start(bf16[512,256]{1,0:T(8,128)(2,1)S(1)} %get-tuple-element.64), channel_id=1, source_target_pairs={{0,1},{1,0},{2,3},{3,2},{4,5},{5,4},{6,7},{7,6},{8,9},{9,8},{10,11... | collective-permute-start | bytes 786440 | tf_op jit(solution)/shard_map/ppermute | solution.py:48
  24.4 9.8 %collective-permute-start.5 = (bf16[2,256,256]{2,1,0:T(8,128)(2,1)S(1)}, bf16[2,256,256]{2,1,0:T(8,128)(2,1)S(1)}, u32[]{:S(2)}, u32[]{:S(2)}) collective-permute-start(bf16[2,256,256]{2,1,0:T(8,128)(2,1)S(1)} %shard_map.76), channel_id=1, source_target_pairs={{0,128},{1,129},{2,130},{3,131},{4,132},{5,133},{6,134},{7,135},{8... | collective-permute-start | bytes 786440 | tf_op jit(solution)/shard_map/ppermute | solution.py:48
  25.9 9.3 %collective-permute-start.4 = (bf16[2,256,256]{2,1,0:T(8,128)(2,1)S(1)}, bf16[2,256,256]{2,1,0:T(8,128)(2,1)S(1)}, u32[]{:S(2)}, u32[]{:S(2)}) collective-permute-start(bf16[2,256,256]{2,1,0:T(8,128)(2,1)S(1)} %shard_map.76), channel_id=1, source_target_pairs={{0,192},{1,193},{2,194},{3,195},{4,196},{5,197},{6,198},{7,199},{8... | collective-permute-start | bytes 786440 | tf_op jit(solution)/shard_map/ppermute | solution.py:48
  30.0 6.4 %collective-permute-start.3 = (bf16[2,256,256]{2,1,0:T(8,128)(2,1)S(1)}, bf16[2,256,256]{2,1,0:T(8,128)(2,1)S(1)}, u32[]{:S(2)}, u32[]{:S(2)}) collective-permute-start(bf16[2,256,256]{2,1,0:T(8,128)(2,1)S(1)} %shard_map.76), channel_id=1, source_target_pairs={{0,64},{1,65},{2,66},{3,67},{4,68},{5,69},{6,70},{7,71},{8,72},{9,... | collective-permute-start | bytes 786440 | tf_op jit(solution)/shard_map/ppermute | solution.py:48
  36.5 11.4 %collective-permute-start.11 = (bf16[2,1024,256]{2,1,0:T(8,128)(2,1)S(1)}, bf16[2,1024,256]{2,1,0:T(8,128)(2,1)S(1)}, u32[]{:S(2)}, u32[]{:S(2)}) collective-permute-start(bf16[2,1024,256]{2,1,0:T(8,128)(2,1)S(1)} %bitcast.12), channel_id=1, source_target_pairs={{0,16},{1,17},{2,18},{3,19},{4,20},{5,21},{6,22},{7,23},{8,24},{9,... | collective-permute-start | bytes 3145736 | tf_op jit(solution)/shard_map/ppermute | solution.py:48
  36.6 19.4 %collective-permute-start.10 = (bf16[8,256,256]{2,1,0:T(8,128)(2,1)S(1)}, bf16[8,256,256]{2,1,0:T(8,128)(2,1)S(1)}, u32[]{:S(2)}, u32[]{:S(2)}) collective-permute-start(bf16[8,256,256]{2,1,0:T(8,128)(2,1)S(1)} %pad_maximum_fusion.refs_0_), channel_id=1, source_target_pairs={{0,12},{1,13},{2,14},{3,15},{4,0},{5,1},{6,2},{7,3},{8,4},{9,5},{1... | collective-permute-start | bytes 3145736 | tf_op jit(solution)/shard_map/ppermute | solution.py:48
  39.7 16.3 %collective-permute-start.9 = (bf16[8,256,256]{2,1,0:T(8,128)(2,1)S(1)}, bf16[8,256,256]{2,1,0:T(8,128)(2,1)S(1)}, u32[]{:S(2)}, u32[]{:S(2)}) collective-permute-start(bf16[8,256,256]{2,1,0:T(8,128)(2,1)S(1)} %pad_maximum_fusion.refs_0_), channel_id=1, source_target_pairs={{0,4},{1,5},{2,6},{3,7},{4,8},{5,9},{6,10},{7,11},{8,12},{9,13},{1... | collective-permute-start | bytes 3145736 | tf_op jit(solution)/shard_map/ppermute | solution.py:48
  56.1 29.8 %collective-permute-start.12 = (bf16[4,256,256]{2,1,0:T(8,128)(2,1)S(1)}, bf16[4,256,256]{2,1,0:T(8,128)(2,1)S(1)}, u32[]{:S(2)}, u32[]{:S(2)}) collective-permute-start(bf16[4,256,256]{2,1,0:T(8,128)(2,1)S(1)} %slice.22), channel_id=1, source_target_pairs={{0,4},{1,5},{2,6},{3,7},{4,8},{5,9},{6,10},{7,11},{8,12},{9,13},{1... | collective-permute-start | bytes 1572872 | tf_op jit(solution)/shard_map/ppermute | solution.py:48
  56.7 29.2 %collective-permute-start.13 = (bf16[4,256,256]{2,1,0:T(8,128)(2,1)S(1)}, bf16[4,256,256]{2,1,0:T(8,128)(2,1)S(1)}, u32[]{:S(2)}, u32[]{:S(2)}) collective-permute-start(bf16[4,256,256]{2,1,0:T(8,128)(2,1)S(1)} %slice.23), channel_id=1, source_target_pairs={{0,12},{1,13},{2,14},{3,15},{4,0},{5,1},{6,2},{7,3},{8,4},{9,5},{1... | collective-permute-start | bytes 1572872 | tf_op jit(solution)/shard_map/ppermute | solution.py:48
  94.4 8.9 %collective-permute-start.14 = (bf16[4,528,256]{2,1,0:T(8,128)(2,1)S(1)}, bf16[4,528,256]{2,1,0:T(8,128)(2,1)S(1)}, u32[]{:S(2)}, u32[]{:S(2)}) collective-permute-start(bf16[4,528,256]{2,1,0:T(8,128)(2,1)S(1)} %get-tuple-element.98), channel_id=1, source_target_pairs={{0,16},{1,17},{2,18},{3,19},{4,20},{5,21},{6,22},{7,23},{8,24},{9,... | collective-permute-start | bytes 3244040 | tf_op jit(solution)/shard_map/ppermute | solution.py:48
  103.3 17.9 %copy-start = (bf16[64,4096]{1,0:T(8,128)(2,1)S(1)}, bf16[64,4096]{1,0:T(8,128)(2,1)}, u32[]{:S(2)}) copy-start(bf16[64,4096]{1,0:T(8,128)(2,1)} %gate.1) | copy-start | bytes 1572868
  103.9 14.8 %collective-permute-start.15 = (bf16[528,256]{1,0:T(8,128)(2,1)S(1)}, bf16[528,256]{1,0:T(8,128)(2,1)S(1)}, u32[]{:S(2)}, u32[]{:S(2)}) collective-permute-start(bf16[528,256]{1,0:T(8,128)(2,1)S(1)} %get-tuple-element.100), channel_id=1, source_target_pairs={{0,1},{1,0},{2,3},{3,2},{4,5},{5,4},{6,7},{7,6},{8,9},{9,8},{10,11... | collective-permute-start | bytes 811016 | tf_op jit(solution)/shard_map/ppermute | solution.py:48
  104.0 14.7 %collective-permute-start.16 = (bf16[528,256]{1,0:T(8,128)(2,1)S(1)}, bf16[528,256]{1,0:T(8,128)(2,1)S(1)}, u32[]{:S(2)}, u32[]{:S(2)}) collective-permute-start(bf16[528,256]{1,0:T(8,128)(2,1)S(1)} %get-tuple-element.101), channel_id=1, source_target_pairs={{0,34},{1,3},{2,0},{3,33},{4,38},{5,7},{6,4},{7,37},{8,42},{9,11},... | collective-permute-start | bytes 811016 | tf_op jit(solution)/shard_map/ppermute | solution.py:48
  108.4 12.7 %collective-permute-start.17 = (bf16[528,256]{1,0:T(8,128)(2,1)S(1)}, bf16[528,256]{1,0:T(8,128)(2,1)S(1)}, u32[]{:S(2)}, u32[]{:S(2)}) collective-permute-start(bf16[528,256]{1,0:T(8,128)(2,1)S(1)} %get-tuple-element.102), channel_id=1, source_target_pairs={{0,35},{1,2},{2,1},{3,32},{4,39},{5,6},{6,5},{7,36},{8,43},{9,10},... | collective-permute-start | bytes 811016 | tf_op jit(solution)/shard_map/ppermute | solution.py:48
  (2 other events, 1.3 us)
where the time goes:
time: 124 us; the launch traced here: 123 us
  Pallas kernels  70.5 us (57%)
  starting transfers between devices  27.1 us (22%)
  waiting for transfers between devices  19.9 us (16%)
  local copies, waits for them, and re-layouts  4.24 us (3%)
    pallas_call x6, Pallas kernels, attend(): pl.pallas_call(functools.partial(attend_kernel, stage, first_tile, len(st...  60 us
    ppermute x18, starting transfers between devices, send(): return lax.ppermute(array, AXES, route)  27.1 us
    ppermute x18, waiting for transfers between devices, send(): return lax.ppermute(array, AXES, route)  19.9 us
    unnamed x16, local copies, waits for them, and re-layouts  4.06 us
    pallas_call x1, Pallas kernels, local(): pl.pallas_call(plan_kernel, in_specs=[SMEM] * 2 + [VMEM] * 2, out_specs=S...  3.53 us
  transfers between devices with their start and end apart: 18, of which 6 were waited for; matrix products, arithmetic and copies ran while one was open for 1% of the time, Pallas kernels for 48%

commit v1 on v0

--- a/solution.py
+++ b/solution.py
@@ -115,7 +115,31 @@
     return (at + 4 - shift) & 3
 
 
-def start_kernel(place, span_of, frequency, starts, angles):
+STAGES = ((0, 8), (8, 8), (16, 8), (24, 8))
+PER_TILE = 72
+NEVER = -(1 << 20)
+
+ORDER = ((0, 0), (0, 4), (1, 0), (3, 4), (1, 4), (3, 0), (2, 0), (2, 4))
+
+
+def prepare_kernel(
+    place,
+    span_of,
+    frequency,
+    gain,
+    k_gain,
+    queries,
+    plan,
+    cosine,
+    sine,
+    own,
+    other,
+    starts,
+    fetched,
+    done,
+):
+    fetch = pltpu.make_async_copy(queries, fetched, done.at[0])
+    fetch.start()
     x, zh, c, y, zl = (place[n] for n in range(5))
     side = zl & 1
 
@@ -130,54 +154,49 @@
             starts[2 * core + n] = first_position(
                 x, at >> 2, c ^ core, y, ((at & 3) >> 1) * CHUNK
             )
-    for a, outer in enumerate(SHIFTS):
-        for b, inner in enumerate(SHIFTS):
+    for a, (outer, low) in enumerate(ORDER):
+        for b in range(4):
+            inner = SHIFTS[(low + b) // 2]
             xs = jnp.where(c == 0, ring_source(x, inner), ring_source(x, outer))
             ys = jnp.where(c == 0, ring_source(y, outer), ring_source(y, inner))
-            for t in range(2):
-                starts[4 + a * 8 + b * 2 + t] = first_position(
-                    xs, zh ^ t, c, ys, (zl >> 1) * CHUNK
-                )
+            starts[4 + a * 4 + b] = first_position(
+                xs, zh ^ (b & 1), c, ys, (zl >> 1) * CHUNK
+            )
+
     row = lax.broadcasted_iota(jnp.int32, (ROWS, 128), 0)
-    firsts = [starts[0] + side * ROWS]
-    firsts += [starts[4 + t] + (side ^ n) * ROWS for t in range(2) for n in range(2)]
-    for n, first in enumerate(firsts):
-        angles[n * ROWS : (n + 1) * ROWS] = (row + first).astype(jnp.float32) * frequency[...]
-
-
-STAGES = ((0, 8), (8, 16), (24, 8))
-PER_TILE = 72
-NEVER = -(1 << 20)
-
-
-def plan_kernel(place, starts, q_gain, k_gain, plan):
-    for tile in range(4):
-        base = tile * PER_TILE
-
-        def clear(n, carry):
-            plan[base + n] = 0
-            plan[base + 32 + n] = NEVER
-            return carry
-
-        lax.fori_loop(0, 32, clear, 0)
+    lane = lax.broadcasted_iota(jnp.int32, (ROWS, 128), 1)
+
+    def rotation(first):
+        angles = (row + first).astype(jnp.float32) * frequency[...]
+        sines = jnp.sin(angles)
+        sines = jnp.where(lane < ROTARY // 2, -sines, sines)
+        rotated = lane < ROTARY
+        return jnp.where(rotated, jnp.cos(angles), 1.0), jnp.where(rotated, sines, 0.0)
+
+    for t in range(2):
+        for n in range(2):
+            rows = slice((2 * t + n) * ROWS, (2 * t + n + 1) * ROWS)
+            cosine[rows], sine[rows] = rotation(starts[4 + t] + (side ^ n) * ROWS)
+    q_cosine, q_sine = rotation(starts[0] + side * ROWS)
+    fetch.wait()
+    for head, out in ((side, own), (1 - side, other)):
+        for member in range(GROUP):
+            columns = pl.ds(pl.multiple_of((head * GROUP + member) * DIM, DIM), DIM)
+            piece = turned(fetched[:, columns], gain[...], q_cosine, q_sine)
+            out[member * ROWS : (member + 1) * ROWS] = piece * jnp.bfloat16(DIM**-0.5)
+
+    for t in range(4):
         for stage, (first, chunks) in enumerate(STAGES):
-
-            def visit(j, count):
-                reach = starts[tile] - starts[4 + first + j]
-                seen = reach > -CHUNK
-                at = base + first + count
-
-                @pl.when(seen)
-                def _():
-                    plan[at] = j
-                    plan[at + 32] = reach
-
-                return count + seen.astype(jnp.int32)
-
-            count = lax.fori_loop(0, chunks, visit, jnp.int32(0))
-            plan[base + 64 + stage] = (count + 3) >> 2
-    plan[4 * PER_TILE] = place[4] & 1
-    bound = jnp.max(jnp.abs(q_gain[...])) * jnp.max(jnp.abs(k_gain[...])) * (16.0 * 1.02 * LOG2E)
+            at = t * PER_TILE + first
+            count = jnp.int32(0)
+            for j in range(chunks):
+                reach = starts[t] - starts[4 + first + j]
+                plan[at + count] = j
+                plan[at + 32 + count] = reach
+                count += (reach > -CHUNK).astype(jnp.int32)
+            plan[t * PER_TILE + 64 + stage] = count
+    plan[4 * PER_TILE] = side
+    bound = jnp.max(jnp.abs(gain[...])) * jnp.max(jnp.abs(k_gain[...])) * (16.0 * 1.02 * LOG2E)
     plan[4 * PER_TILE + 1] = (bound <= 100.0).astype(jnp.int32)
 
 
@@ -189,17 +208,8 @@
         out[t, CHUNK + low : CHUNK + low + ROWS] = piece[ROWS:]
 
 
-def queries_kernel(place, queries, gain, cosine, sine, own, other):
-    side = place[4] & 1
-    for head, out in ((side, own), (1 - side, other)):
-        for member in range(GROUP):
-            columns = pl.ds(pl.multiple_of((head * GROUP + member) * DIM, DIM), DIM)
-            piece = turned(queries[:, columns], gain[...], cosine[...], sine[...])
-            out[member * ROWS : (member + 1) * ROWS] = piece * jnp.bfloat16(DIM**-0.5)
-
-
 def attend_kernel(stage, first_tile, buffers, plan, queries, *refs):
-    first, last = stage == 0, stage == 2
+    first, last = stage == 0, stage == 3
     stores, refs = refs[:buffers], list(refs[buffers:])
     if not first:
         del refs[:3]
@@ -217,18 +227,21 @@
 
     def fetch(j, part):
         rows = slice(part * CHUNK, (part + 1) * CHUNK)
-        if buffers == 1:
-            return stores[0][j, rows]
         within = lax.rem(j, per_store)
-        return jnp.where(j >= per_store, stores[1][within, rows], stores[0][within, rows])
+        picked = stores[0][within, rows]
+        for n in range(1, buffers):
+            picked = jnp.where(j >= n * per_store, stores[n][within, rows], picked)
+        return picked
 
     row = lax.broadcasted_iota(jnp.int32, (TILE, CHUNK), 0)
     lane = lax.broadcasted_iota(jnp.int32, (TILE, CHUNK), 1)
 
     def gather(tile, n):
-        at = (first_tile + tile) * PER_TILE + STAGES[stage][0] + 4 * n
-        picks = [plan[at + m] for m in range(4)]
-        limits = [plan[at + 32 + m] for m in range(4)]
+        base = (first_tile + tile) * PER_TILE
+        at = base + STAGES[stage][0] + 4 * n
+        real = [4 * n + m < plan[base + 64 + stage] for m in range(4)]
+        picks = [jnp.where(real[m], plan[at + m], 0) for m in range(4)]
+        limits = [jnp.where(real[m], plan[at + 32 + m], NEVER) for m in range(4)]
         keys = jnp.concatenate([fetch(j, 0) for j in picks], axis=0)
         values = jnp.concatenate([fetch(j, 1) for j in picks], axis=0)
         return keys, values, limits
@@ -257,7 +270,7 @@
         )
 
     bases = [(first_tile + tile) * PER_TILE for tile in range(2)]
-    steps = jnp.maximum(plan[bases[0] + 64 + stage], plan[bases[1] + 64 + stage])
+    steps = (jnp.maximum(plan[bases[0] + 64 + stage], plan[bases[1] + 64 + stage]) + 3) >> 2
 
     @pl.when(bounded)
     def _():
@@ -371,10 +384,10 @@
     shapes = [
         jax.ShapeDtypeStruct((2, 2 * TILE, width), jnp.float32) for width in (128, 128, DIM)
     ]
-    if stage == 2:
+    if stage == 3:
         shapes = [jax.ShapeDtypeStruct((4, TILE + STATS, DIM), jnp.bfloat16)] + shapes
     given = 2 + len(stores)
-    aliases = {given + n: n + (stage == 2) for n in range(len(state))}
+    aliases = {given + n: n + (stage == 3) for n in range(len(state))}
     chunks = STAGES[stage][1]
     return pl.pallas_call(
         functools.partial(attend_kernel, stage, first_tile, len(stores)),
@@ -399,7 +412,7 @@
     pair = jax.ShapeDtypeStruct((2 * ROWS, DIM), jnp.bfloat16)
     kv_own, kv_other = pl.pallas_call(
         split_kernel,
-        in_specs=[SMEM] + [pl.BlockSpec(memory_space=pl.ANY)] * 2,
+        in_specs=[SMEM] + [pl.BlockSpec(memory_space=pltpu.HBM)] * 2,
         out_specs=[VMEM] * 2,
         out_shape=[pair, pair],
         scratch_shapes=[pltpu.SemaphoreType.DMA((4,))],
@@ -408,33 +421,30 @@
     far = send(kv_own, to_far(0))
     cross = send(kv_other, to_far(1))
     mate = send(kv_other, to_mate)
-    span_of, _ = lax.optimization_barrier((span_of, kv_own))
+    later_place, _ = lax.optimization_barrier((place, kv_own))
 
     lane = jnp.arange(128, dtype=jnp.int32)
     frequency = ROPE_BASE ** (-2.0 * (lane % 32).astype(jnp.float32) / ROTARY)
-    starts, angles = pl.pallas_call(
-        start_kernel,
-        in_specs=[SMEM] * 2 + [VMEM],
-        out_specs=[SMEM, VMEM],
+    tile = jax.ShapeDtypeStruct((TILE, DIM), jnp.bfloat16)
+    table = jax.ShapeDtypeStruct((4 * ROWS, 128), jnp.float32)
+    plan, cosine, sine, q_own, q_other = pl.pallas_call(
+        prepare_kernel,
+        in_specs=[SMEM] * 2 + [VMEM] * 3 + [pl.BlockSpec(memory_space=pltpu.HBM)],
+        out_specs=[SMEM] + [VMEM] * 4,
         out_shape=[
-            jax.ShapeDtypeStruct((36,), jnp.int32),
-            jax.ShapeDtypeStruct((5 * ROWS, 128), jnp.float32),
+            jax.ShapeDtypeStruct((4 * PER_TILE + 8,), jnp.int32),
+            table,
+            table,
+            tile,
+            tile,
+        ],
+        scratch_shapes=[
+            pltpu.SMEM((36,), jnp.int32),
+            pltpu.VMEM(queries.shape, jnp.bfloat16),
+            pltpu.SemaphoreType.DMA((1,)),
         ],
         compiler_params=BIG,
-    )(place, span_of, frequency.reshape(1, 128))
-    rotated = lane[None, :] < ROTARY
-    cosine = jnp.where(rotated, jnp.cos(angles), 1.0)
-    sine = jnp.sin(angles)
-    sine = jnp.where(rotated, jnp.where(lane[None, :] < ROTARY // 2, -sine, sine), 0.0)
-
-    tile = jax.ShapeDtypeStruct((TILE, DIM), jnp.bfloat16)
-    q_own, q_other = pl.pallas_call(
-        queries_kernel,
-        in_specs=[SMEM] + [VMEM] * 4,
-        out_specs=[VMEM] * 2,
-        out_shape=[tile, tile],
-        compiler_params=BIG,
-    )(place, queries, q_gain, cosine[:ROWS], sine[:ROWS])
+    )(later_place, span_of, frequency.reshape(1, 128), q_gain, k_gain, queries)
     mate, far, cross, q_own, q_other = lax.optimization_barrier((mate, far, cross, q_own, q_other))
 
     base = pl.pallas_call(
@@ -443,38 +453,33 @@
         out_specs=VMEM,
         out_shape=jax.ShapeDtypeStruct((2, 2 * CHUNK, DIM), jnp.bfloat16),
         compiler_params=BIG,
-    )(kv_own, mate, far, cross, k_gain, cosine[ROWS:], sine[ROWS:])
-
-    plan = pl.pallas_call(
-        plan_kernel,
-        in_specs=[SMEM] * 2 + [VMEM] * 2,
-        out_specs=SMEM,
-        out_shape=jax.ShapeDtypeStruct((4 * PER_TILE + 8,), jnp.int32),
-        compiler_params=BIG,
-    )(place, starts, q_gain, k_gain)
-
-    store = [base] + [send(base, to_ring(s, 0)) for s in SHIFTS[1:]]
-    store = jnp.concatenate(store, axis=0)
+    )(kv_own, mate, far, cross, k_gain, cosine, sine)
+
+    rings = [base] + [send(base, to_ring(s, 0)) for s in SHIFTS[1:]]
+    low, high = jnp.concatenate(rings[:2], axis=0), jnp.concatenate(rings[2:], axis=0)
+
     q_mine = jnp.stack(
         [q_own, send(q_other, to_mate), send(q_own, along_z(2)), send(q_other, along_z(-1))]
     ).reshape(2, 2 * TILE, DIM)
-    store, q_mine, plan = lax.optimization_barrier((store, q_mine, plan))
+    low, high, q_mine = lax.optimization_barrier((low, high, q_mine))
     q_theirs = send(q_mine, to_core)
-    arrived = [send(store, to_ring(s, 1)) for s in SHIFTS[1:3]]
-    mine = attend(plan, q_mine, [store], [], 0, 0)
-    theirs = attend(plan, q_theirs, [store], [], 0, 2)
-
-    arrived, mine, theirs = lax.optimization_barrier((arrived, mine, theirs))
-    last = [
-        send(arrived[0][:4], to_ring(1, 1)),
-        send(arrived[1][4:], to_ring(3, 1)),
-    ]
-    mine = attend(plan, q_mine, arrived, mine, 1, 0)
-    theirs = attend(plan, q_theirs, arrived, theirs, 1, 2)
+    first = [send(low, to_ring(1, 1)), send(high, to_ring(3, 1))]
+    mine = attend(plan, q_mine, [low, high], [], 0, 0)
+    low, high, mine = lax.optimization_barrier((low, high, mine))
+    second = [send(high, to_ring(1, 1)), send(low, to_ring(3, 1))]
+    theirs = attend(plan, q_theirs, [low, high], [], 0, 2)
+
+    first, mine, theirs = lax.optimization_barrier((first, mine, theirs))
+    last = [send(first[0], to_ring(1, 1)), send(first[1], to_ring(3, 1))]
+    mine = attend(plan, q_mine, first, mine, 1, 0)
+    theirs = attend(plan, q_theirs, first, theirs, 1, 2)
+    second, mine, theirs = lax.optimization_barrier((second, mine, theirs))
+    mine = attend(plan, q_mine, second, mine, 2, 0)
+    theirs = attend(plan, q_theirs, second, theirs, 2, 2)
     last, mine, theirs = lax.optimization_barrier((last, mine, theirs))
-    out_theirs = attend(plan, q_theirs, last, theirs, 2, 2)[0]
+    out_theirs = attend(plan, q_theirs, last, theirs, 3, 2)[0]
     received = send(out_theirs, to_core)
-    out_mine = attend(plan, q_mine, last, mine, 2, 0)[0]
+    out_mine = attend(plan, q_mine, last, mine, 3, 0)[0]
 
     joint = jax.ShapeDtypeStruct((TILE + STATS, DIM), jnp.bfloat16)
     parts = pl.pallas_call(

time: 124 us -> 130 us (1.048)
  the two profiles are of different devices: /device:TPU:6 before, /device:TPU:4 now
where the time goes in v1:
time: 130 us; the launch traced here: 129 us
  Pallas kernels  71.8 us (55%)
  starting transfers between devices  31.2 us (24%)
  waiting for transfers between devices  21 us (16%)
  local copies, waits for them, and re-layouts  4.82 us (4%)
    pallas_call x8, Pallas kernels, attend(): pl.pallas_call(functools.partial(attend_kernel, stage, first_tile, len(st...  64.5 us
    ppermute x20, starting transfers between devices, send(): return lax.ppermute(array, AXES, route)  31.2 us
    ppermute x20, waiting for transfers between devices, send(): return lax.ppermute(array, AXES, route)  21 us
    unnamed x14, local copies, waits for them, and re-layouts  4.74 us
    pallas_call x1, Pallas kernels, local(): pl.pallas_call(prepare_kernel, in_specs=[SMEM] * 2 + [VMEM] * 3 + [pl.Blo...  3.96 us
  transfers between devices with their start and end apart: 20, of which 6 were waited for; matrix products, arithmetic and copies ran while one was open for 0% of the time, Pallas kernels for 46%

profile of v1, /device:TPU:4, one launch (start us, length us, event | category | flops | bytes accessed | tf_op | source)
XLA Modules:
  0.0 129.3 jit_solution(5186515197349145372)
XLA Ops:
  2.4 2.0 %collective-permute-start = (bf16[128,256]{1,0:T(8,128)(2,1)S(1)}, bf16[128,256]{1,0:T(8,128)(2,1)S(1)}, u32[]{:S(2)}, u32[]{:S(2)}) collective-permute-start(bf16[128,256]{1,0:T(8,128)(2,1)S(1)} %get-tuple-element.77), channel_id=1, source_target_pairs={{0,1},{1,0},{2,3},{3,2},{4,5},{5,4},{6,7},{7,6},{8,9},{9,8},{10,11... | collective-permute-start | bytes 196616 | tf_op jit(solution)/shard_map/ppermute | solution.py:48
  4.4 5.8 %collective-permute-start.2 = (bf16[128,256]{1,0:T(8,128)(2,1)S(1)}, bf16[128,256]{1,0:T(8,128)(2,1)S(1)}, u32[]{:S(2)}, u32[]{:S(2)}) collective-permute-start(bf16[128,256]{1,0:T(8,128)(2,1)S(1)} %get-tuple-element.77), channel_id=1, source_target_pairs={{0,33},{1,32},{2,35},{3,34},{4,37},{5,36},{6,39},{7,38},{8,41},{9,... | collective-permute-start | bytes 196616 | tf_op jit(solution)/shard_map/ppermute | solution.py:48
  13.8 4.0 %shard_map.74 = (s32[296]{0:T(512)S(1)}, f32[256,128]{1,0:T(8,128)S(1)}, f32[256,128]{1,0:T(8,128)S(1)}, bf16[512,256]{1,0:T(8,128)(2,1)S(1)}, bf16[512,256]{1,0:T(8,128)(2,1)S(1)}) custom-call(s32[5]{0:T(128)S(1)} %stack.38.place, s32[32]{0:T(128)S(1)} %copy-done.6, f32[1,128]{1,0:T(1,128)S(1)} %fusion.2.frequency, f32[1,256]{1,0:T(1,128)S(1)} %bitcast.20, ...), custom_call_target="tpu_custom_call" | custom-call | tf_op jit(solution)/shard_map/pallas_call | solution.py:430
  20.6 2.9 %collective-permute-start.8 = (bf16[512,256]{1,0:T(8,128)(2,1)S(1)}, bf16[512,256]{1,0:T(8,128)(2,1)S(1)}, u32[]{:S(2)}, u32[]{:S(2)}) collective-permute-start(bf16[512,256]{1,0:T(8,128)(2,1)S(1)} %get-tuple-element.86), channel_id=1, source_target_pairs={{0,35},{1,2},{2,1},{3,32},{4,39},{5,6},{6,5},{7,36},{8,43},{9,10},... | collective-permute-start | bytes 786440 | tf_op jit(solution)/shard_map/ppermute | solution.py:48
  23.5 2.5 %collective-permute-start.7 = (bf16[512,256]{1,0:T(8,128)(2,1)S(1)}, bf16[512,256]{1,0:T(8,128)(2,1)S(1)}, u32[]{:S(2)}, u32[]{:S(2)}) collective-permute-start(bf16[512,256]{1,0:T(8,128)(2,1)S(1)} %get-tuple-element.85), channel_id=1, source_target_pairs={{0,2},{1,35},{2,32},{3,1},{4,6},{5,39},{6,36},{7,5},{8,10},{9,43},... | collective-permute-start | bytes 786440 | tf_op jit(solution)/shard_map/ppermute | solution.py:48
  26.8 1.7 %collective-permute-start.5 = (bf16[2,256,256]{2,1,0:T(8,128)(2,1)S(1)}, bf16[2,256,256]{2,1,0:T(8,128)(2,1)S(1)}, u32[]{:S(2)}, u32[]{:S(2)}) collective-permute-start(bf16[2,256,256]{2,1,0:T(8,128)(2,1)S(1)} %shard_map.75), channel_id=1, source_target_pairs={{0,128},{1,129},{2,130},{3,131},{4,132},{5,133},{6,134},{7,135},{8... | collective-permute-start | bytes 786440 | tf_op jit(solution)/shard_map/ppermute | solution.py:48
  30.1 2.6 %collective-permute-done.6 = bf16[512,256]{1,0:T(8,128)(2,1)S(1)} collective-permute-done((bf16[512,256]{1,0:T(8,128)(2,1)S(1)}, bf16[512,256]{1,0:T(8,128)(2,1)S(1)}, u32[]{:S(2)}, u32[]{:S(2)}) %collective-permute-start.6) | collective-permute-done | bytes 262176 | tf_op jit(solution)/shard_map/ppermute | solution.py:48
  32.7 3.1 %collective-permute-done.7 = bf16[512,256]{1,0:T(8,128)(2,1)S(1)} collective-permute-done((bf16[512,256]{1,0:T(8,128)(2,1)S(1)}, bf16[512,256]{1,0:T(8,128)(2,1)S(1)}, u32[]{:S(2)}, u32[]{:S(2)}) %collective-permute-start.7) | collective-permute-done | bytes 262176 | tf_op jit(solution)/shard_map/ppermute | solution.py:48
  36.2 2.0 %collective-permute-start.10 = (bf16[4,256,256]{2,1,0:T(8,128)(2,1)S(1)}, bf16[4,256,256]{2,1,0:T(8,128)(2,1)S(1)}, u32[]{:S(2)}, u32[]{:S(2)}) collective-permute-start(bf16[4,256,256]{2,1,0:T(8,128)(2,1)S(1)} %pad_maximum_fusion.2.refs_1_), channel_id=1, source_target_pairs={{0,12},{1,13},{2,14},{3,15},{4,0},{5,1},{6,2},{7,3},{8,4},{9,5},{1... | collective-permute-start | bytes 1572872 | tf_op jit(solution)/shard_map/ppermute | solution.py:48
  38.3 8.2 %shard_map.76 = (f32[2,1024,128]{2,1,0:T(8,128)S(1)}, f32[2,1024,128]{2,1,0:T(8,128)S(1)}, f32[2,1024,256]{2,1,0:T(8,128)S(1)}) custom-call(s32[296]{0:T(512)S(1)} %get-tuple-element.76.plan, bf16[2,1024,256]{2,1,0:T(8,128)(2,1)S(1)} %bitcast.13, bf16[4,256,256]{2,1,0:T(8,128)(2,1)S(1)} %pad_maximum_fusion.1.refs_0_, ...), custom_call_target="tpu_custom_call" | custom-call | flops 2147483648 | bytes 4194304 | tf_op jit(solution)/shard_map/pallas_call | solution.py:392
  46.5 1.7 %collective-permute-start.14 = (bf16[4,256,256]{2,1,0:T(8,128)(2,1)S(1)}, bf16[4,256,256]{2,1,0:T(8,128)(2,1)S(1)}, u32[]{:S(2)}, u32[]{:S(2)}) collective-permute-start(bf16[4,256,256]{2,1,0:T(8,128)(2,1)S(1)} %pad_maximum_fusion.2.refs_1_), channel_id=1, source_target_pairs={{0,4},{1,5},{2,6},{3,7},{4,8},{5,9},{6,10},{7,11},{8,12},{9,13},{1... | collective-permute-start | bytes 1572872 | tf_op jit(solution)/shard_map/ppermute | solution.py:48
  48.1 1.7 %collective-permute-start.15 = (bf16[4,256,256]{2,1,0:T(8,128)(2,1)S(1)}, bf16[4,256,256]{2,1,0:T(8,128)(2,1)S(1)}, u32[]{:S(2)}, u32[]{:S(2)}) collective-permute-start(bf16[4,256,256]{2,1,0:T(8,128)(2,1)S(1)} %pad_maximum_fusion.1.refs_0_), channel_id=1, source_target_pairs={{0,12},{1,13},{2,14},{3,15},{4,0},{5,1},{6,2},{7,3},{8,4},{9,5},{1... | collective-permute-start | bytes 1572872 | tf_op jit(solution)/shard_map/ppermute | solution.py:48
  49.8 8.1 %shard_map.77 = (f32[2,1024,128]{2,1,0:T(8,128)S(1)}, f32[2,1024,128]{2,1,0:T(8,128)S(1)}, f32[2,1024,256]{2,1,0:T(8,128)S(1)}) custom-call(s32[296]{0:T(512)S(1)} %get-tuple-element.76.plan, bf16[2,1024,256]{2,1,0:T(8,128)(2,1)S(1)} %collective-permute-done.11.queries, bf16[4,256,256]{2,1,0:T(8,128)(2,1)S(1)} %pad_maximum_fusion.1.refs_0_, ...), custom_call_target="tpu_custom_call" | custom-call | flops 2147483648 | bytes 4194304 | tf_op jit(solution)/shard_map/pallas_call | solution.py:392
  58.4 2.9 %collective-permute-start.13 = (bf16[4,256,256]{2,1,0:T(8,128)(2,1)S(1)}, bf16[4,256,256]{2,1,0:T(8,128)(2,1)S(1)}, u32[]{:S(2)}, u32[]{:S(2)}) collective-permute-start(bf16[4,256,256]{2,1,0:T(8,128)(2,1)S(1)} %collective-permute-done.10.refs_1_), channel_id=1, source_target_pairs={{0,12},{1,13},{2,14},{3,15},{4,0},{5,1},{6,2},{7,3},{8,4},{9,5},{1... | collective-permute-start | bytes 1572872 | tf_op jit(solution)/shard_map/ppermute | solution.py:48
  61.2 7.8 %shard_map.78 = (f32[2,1024,128]{2,1,0:T(8,128)S(1)}, f32[2,1024,128]{2,1,0:T(8,128)S(1)}, f32[2,1024,256]{2,1,0:T(8,128)S(1)}) custom-call(s32[296]{0:T(512)S(1)} %get-tuple-element.76.plan, bf16[2,1024,256]{2,1,0:T(8,128)(2,1)S(1)} %bitcast.14, ...), custom_call_target="tpu_custom_call", output_to_operand_aliasing={{0}: (4, {}), {1}: (5, {}), {2}: (6, {})} | custom-call | flops 2147483648 | bytes 4194304 | tf_op jit(solution)/shard_map/pallas_call | solution.py:392
  69.0 7.8 %shard_map.79 = (f32[2,1024,128]{2,1,0:T(8,128)S(1)}, f32[2,1024,128]{2,1,0:T(8,128)S(1)}, f32[2,1024,256]{2,1,0:T(8,128)S(1)}) custom-call(s32[296]{0:T(512)S(1)} %get-tuple-element.76.plan, bf16[2,1024,256]{2,1,0:T(8,128)(2,1)S(1)} %collective-permute-done.11.queries, ...), custom_call_target="tpu_custom_call", output_to_operand_aliasing={{0}: (4, {}), {1}: (5, {}), {2}: (6, {})} | custom-call | flops 2147483648 | bytes 4194304 | tf_op jit(solution)/shard_map/pallas_call | solution.py:392
  76.9 7.8 %shard_map.80 = (f32[2,1024,128]{2,1,0:T(8,128)S(1)}, f32[2,1024,128]{2,1,0:T(8,128)S(1)}, f32[2,1024,256]{2,1,0:T(8,128)S(1)}) custom-call(s32[296]{0:T(512)S(1)} %get-tuple-element.76.plan, bf16[2,1024,256]{2,1,0:T(8,128)(2,1)S(1)} %bitcast.15, ...), custom_call_target="tpu_custom_call", output_to_operand_aliasing={{0}: (4, {}), {1}: (5, {}), {2}: (6, {})} | custom-call | flops 2147483648 | bytes 4194304 | tf_op jit(solution)/shard_map/pallas_call | solution.py:392
  84.6 8.1 %shard_map.81 = (f32[2,1024,128]{2,1,0:T(8,128)S(1)}, f32[2,1024,128]{2,1,0:T(8,128)S(1)}, f32[2,1024,256]{2,1,0:T(8,128)S(1)}) custom-call(s32[296]{0:T(512)S(1)} %get-tuple-element.76.plan, bf16[2,1024,256]{2,1,0:T(8,128)(2,1)S(1)} %collective-permute-done.11.queries, ...), custom_call_target="tpu_custom_call", output_to_operand_aliasing={{0}: (4, {}), {1}: (5, {}), {2}: (6, {})} | custom-call | flops 2147483648 | bytes 4194304 | tf_op jit(solution)/shard_map/pallas_call | solution.py:392
  92.7 8.4 %shard_map.83 = (bf16[4,528,256]{2,1,0:T(8,128)(2,1)S(1)}, f32[2,1024,128]{2,1,0:T(8,128)S(1)}, f32[2,1024,128]{2,1,0:T(8,128)S(1)}, f32[2,1024,256]{2,1,0:T(8,128)S(1)}) custom-call(s32[296]{0:T(512)S(1)} %get-tuple-element.76.plan, ...), custom_call_target="tpu_custom_call", output_to_operand_aliasing={{1}: (4, {}), {2}: (5, {}), {3}: (6, {})} | custom-call | flops 2147483648 | bytes 4194304 | tf_op jit(solution)/shard_map/pallas_call | solution.py:392
  101.2 8.4 %shard_map.82 = (bf16[4,528,256]{2,1,0:T(8,128)(2,1)S(1)}, f32[2,1024,128]{2,1,0:T(8,128)S(1)}, f32[2,1024,128]{2,1,0:T(8,128)S(1)}, f32[2,1024,256]{2,1,0:T(8,128)S(1)}) custom-call(s32[296]{0:T(512)S(1)} %get-tuple-element.76.plan, bf16[2,1024,256]{2,1,0:T(8,128)(2,1)S(1)} %bitcast.16, ...), custom_call_target="tpu_custom_call", output_to_operand_aliasing={{1}: (4, {}), {2}: (5, {}), {3}: (6, {})} | custom-call | flops 2147483648 | bytes 4194304 | tf_op jit(solution)/shard_map/pallas_call | solution.py:392
  110.4 4.4 %collective-permute-start.18 = (bf16[528,256]{1,0:T(8,128)(2,1)S(1)}, bf16[528,256]{1,0:T(8,128)(2,1)S(1)}, u32[]{:S(2)}, u32[]{:S(2)}) collective-permute-start(bf16[528,256]{1,0:T(8,128)(2,1)S(1)} %get-tuple-element.141), channel_id=1, source_target_pairs={{0,34},{1,3},{2,0},{3,33},{4,38},{5,7},{6,4},{7,37},{8,42},{9,11},... | collective-permute-start | bytes 811016 | tf_op jit(solution)/shard_map/ppermute | solution.py:48
  115.1 10.0 %collective-permute-done.17.near1 = bf16[528,256]{1,0:T(8,128)(2,1)S(1)} collective-permute-done((bf16[528,256]{1,0:T(8,128)(2,1)S(1)}, bf16[528,256]{1,0:T(8,128)(2,1)S(1)}, u32[]{:S(2)}, u32[]{:S(2)}) %collective-permute-start.17) | collective-permute-done | bytes 270368 | tf_op jit(solution)/shard_map/ppermute | solution.py:48
  125.0 2.4 %collective-permute-done.19.far1 = bf16[528,256]{1,0:T(8,128)(2,1)S(1)} collective-permute-done((bf16[528,256]{1,0:T(8,128)(2,1)S(1)}, bf16[528,256]{1,0:T(8,128)(2,1)S(1)}, u32[]{:S(2)}, u32[]{:S(2)}) %collective-permute-start.19) | collective-permute-done | bytes 270368 | tf_op jit(solution)/shard_map/ppermute | solution.py:48
  127.5 1.8 %shard_map.85 = bf16[64,4096]{1,0:T(8,128)(2,1)} custom-call(s32[5]{0:T(128)S(1)} %stack.38.place, bf16[528,256]{1,0:T(8,128)(2,1)S(1)} %get-tuple-element.139.near0, bf16[528,256]{1,0:T(8,128)(2,1)S(1)} %collective-permute-done.17.near1, bf16[528,256]{1,0:T(8,128)(2,1)S(1)} %collective-permute-done.18.far0, ...), custom_call_target="tpu_custom_call" | custom-call | tf_op jit(solution)/shard_map/pallas_call | solution.py:499
  (48 shorter events, 13.1 us)
Async XLA Ops:
  0.1 0.8 copy-start.2
  0.9 0.8 copy-start.3
  2.4 15.3 %collective-permute-start = (bf16[128,256]{1,0:T(8,128)(2,1)S(1)}, bf16[128,256]{1,0:T(8,128)(2,1)S(1)}, u32[]{:S(2)}, u32[]{:S(2)}) collective-permute-start(bf16[128,256]{1,0:T(8,128)(2,1)S(1)} %get-tuple-element.77), channel_id=1, source_target_pairs={{0,1},{1,0},{2,3},{3,2},{4,5},{5,4},{6,7},{7,6},{8,9},{9,8},{10,11... | collective-permute-start | bytes 196616 | tf_op jit(solution)/shard_map/ppermute | solution.py:48
  4.4 14.6 %collective-permute-start.2 = (bf16[128,256]{1,0:T(8,128)(2,1)S(1)}, bf16[128,256]{1,0:T(8,128)(2,1)S(1)}, u32[]{:S(2)}, u32[]{:S(2)}) collective-permute-start(bf16[128,256]{1,0:T(8,128)(2,1)S(1)} %get-tuple-element.77), channel_id=1, source_target_pairs={{0,33},{1,32},{2,35},{3,34},{4,37},{5,36},{6,39},{7,38},{8,41},{9,... | collective-permute-start | bytes 196616 | tf_op jit(solution)/shard_map/ppermute | solution.py:48
  10.2 8.7 %collective-permute-start.1 = (bf16[128,256]{1,0:T(8,128)(2,1)S(1)}, bf16[128,256]{1,0:T(8,128)(2,1)S(1)}, u32[]{:S(2)}, u32[]{:S(2)}) collective-permute-start(bf16[128,256]{1,0:T(8,128)(2,1)S(1)} %get-tuple-element.74.own), channel_id=1, source_target_pairs={{0,32},{1,33},{2,34},{3,35},{4,36},{5,37},{6,38},{7,39},{8,40},{9,... | collective-permute-start | bytes 196616 | tf_op jit(solution)/shard_map/ppermute | solution.py:48
  10.7 1.0 copy-start.1
  19.3 7.5 %collective-permute-start.3 = (bf16[2,256,256]{2,1,0:T(8,128)(2,1)S(1)}, bf16[2,256,256]{2,1,0:T(8,128)(2,1)S(1)}, u32[]{:S(2)}, u32[]{:S(2)}) collective-permute-start(bf16[2,256,256]{2,1,0:T(8,128)(2,1)S(1)} %shard_map.75), channel_id=1, source_target_pairs={{0,64},{1,65},{2,66},{3,67},{4,68},{5,69},{6,70},{7,71},{8,72},{9,... | collective-permute-start | bytes 786440 | tf_op jit(solution)/shard_map/ppermute | solution.py:48
  20.6 9.6 %collective-permute-start.8 = (bf16[512,256]{1,0:T(8,128)(2,1)S(1)}, bf16[512,256]{1,0:T(8,128)(2,1)S(1)}, u32[]{:S(2)}, u32[]{:S(2)}) collective-permute-start(bf16[512,256]{1,0:T(8,128)(2,1)S(1)} %get-tuple-element.86), channel_id=1, source_target_pairs={{0,35},{1,2},{2,1},{3,32},{4,39},{5,6},{6,5},{7,36},{8,43},{9,10},... | collective-permute-start | bytes 786440 | tf_op jit(solution)/shard_map/ppermute | solution.py:48
  23.5 9.2 %collective-permute-start.6 = (bf16[512,256]{1,0:T(8,128)(2,1)S(1)}, bf16[512,256]{1,0:T(8,128)(2,1)S(1)}, u32[]{:S(2)}, u32[]{:S(2)}) collective-permute-start(bf16[512,256]{1,0:T(8,128)(2,1)S(1)} %get-tuple-element.86), channel_id=1, source_target_pairs={{0,1},{1,0},{2,3},{3,2},{4,5},{5,4},{6,7},{7,6},{8,9},{9,8},{10,11... | collective-permute-start | bytes 786440 | tf_op jit(solution)/shard_map/ppermute | solution.py:48
  23.5 12.4 %collective-permute-start.7 = (bf16[512,256]{1,0:T(8,128)(2,1)S(1)}, bf16[512,256]{1,0:T(8,128)(2,1)S(1)}, u32[]{:S(2)}, u32[]{:S(2)}) collective-permute-start(bf16[512,256]{1,0:T(8,128)(2,1)S(1)} %get-tuple-element.85), channel_id=1, source_target_pairs={{0,2},{1,35},{2,32},{3,1},{4,6},{5,39},{6,36},{7,5},{8,10},{9,43},... | collective-permute-start | bytes 786440 | tf_op jit(solution)/shard_map/ppermute | solution.py:48
  26.0 10.0 %collective-permute-start.4 = (bf16[2,256,256]{2,1,0:T(8,128)(2,1)S(1)}, bf16[2,256,256]{2,1,0:T(8,128)(2,1)S(1)}, u32[]{:S(2)}, u32[]{:S(2)}) collective-permute-start(bf16[2,256,256]{2,1,0:T(8,128)(2,1)S(1)} %shard_map.75), channel_id=1, source_target_pairs={{0,192},{1,193},{2,194},{3,195},{4,196},{5,197},{6,198},{7,199},{8... | collective-permute-start | bytes 786440 | tf_op jit(solution)/shard_map/ppermute | solution.py:48
  26.8 9.2 %collective-permute-start.5 = (bf16[2,256,256]{2,1,0:T(8,128)(2,1)S(1)}, bf16[2,256,256]{2,1,0:T(8,128)(2,1)S(1)}, u32[]{:S(2)}, u32[]{:S(2)}) collective-permute-start(bf16[2,256,256]{2,1,0:T(8,128)(2,1)S(1)} %shard_map.75), channel_id=1, source_target_pairs={{0,128},{1,129},{2,130},{3,131},{4,132},{5,133},{6,134},{7,135},{8... | collective-permute-start | bytes 786440 | tf_op jit(solution)/shard_map/ppermute | solution.py:48
  36.1 13.7 %collective-permute-start.11 = (bf16[2,1024,256]{2,1,0:T(8,128)(2,1)S(1)}, bf16[2,1024,256]{2,1,0:T(8,128)(2,1)S(1)}, u32[]{:S(2)}, u32[]{:S(2)}) collective-permute-start(bf16[2,1024,256]{2,1,0:T(8,128)(2,1)S(1)} %bitcast.12), channel_id=1, source_target_pairs={{0,16},{1,17},{2,18},{3,19},{4,20},{5,21},{6,22},{7,23},{8,24},{9,... | collective-permute-start | bytes 3145736 | tf_op jit(solution)/shard_map/ppermute | solution.py:48
  36.2 21.7 %collective-permute-start.10 = (bf16[4,256,256]{2,1,0:T(8,128)(2,1)S(1)}, bf16[4,256,256]{2,1,0:T(8,128)(2,1)S(1)}, u32[]{:S(2)}, u32[]{:S(2)}) collective-permute-start(bf16[4,256,256]{2,1,0:T(8,128)(2,1)S(1)} %pad_maximum_fusion.2.refs_1_), channel_id=1, source_target_pairs={{0,12},{1,13},{2,14},{3,15},{4,0},{5,1},{6,2},{7,3},{8,4},{9,5},{1... | collective-permute-start | bytes 1572872 | tf_op jit(solution)/shard_map/ppermute | solution.py:48
  38.2 19.7 %collective-permute-start.9 = (bf16[4,256,256]{2,1,0:T(8,128)(2,1)S(1)}, bf16[4,256,256]{2,1,0:T(8,128)(2,1)S(1)}, u32[]{:S(2)}, u32[]{:S(2)}) collective-permute-start(bf16[4,256,256]{2,1,0:T(8,128)(2,1)S(1)} %pad_maximum_fusion.1.refs_0_), channel_id=1, source_target_pairs={{0,4},{1,5},{2,6},{3,7},{4,8},{5,9},{6,10},{7,11},{8,12},{9,13},{1... | collective-permute-start | bytes 1572872 | tf_op jit(solution)/shard_map/ppermute | solution.py:48
  46.5 30.4 %collective-permute-start.14 = (bf16[4,256,256]{2,1,0:T(8,128)(2,1)S(1)}, bf16[4,256,256]{2,1,0:T(8,128)(2,1)S(1)}, u32[]{:S(2)}, u32[]{:S(2)}) collective-permute-start(bf16[4,256,256]{2,1,0:T(8,128)(2,1)S(1)} %pad_maximum_fusion.2.refs_1_), channel_id=1, source_target_pairs={{0,4},{1,5},{2,6},{3,7},{4,8},{5,9},{6,10},{7,11},{8,12},{9,13},{1... | collective-permute-start | bytes 1572872 | tf_op jit(solution)/shard_map/ppermute | solution.py:48
  48.1 28.7 %collective-permute-start.15 = (bf16[4,256,256]{2,1,0:T(8,128)(2,1)S(1)}, bf16[4,256,256]{2,1,0:T(8,128)(2,1)S(1)}, u32[]{:S(2)}, u32[]{:S(2)}) collective-permute-start(bf16[4,256,256]{2,1,0:T(8,128)(2,1)S(1)} %pad_maximum_fusion.1.refs_0_), channel_id=1, source_target_pairs={{0,12},{1,13},{2,14},{3,15},{4,0},{5,1},{6,2},{7,3},{8,4},{9,5},{1... | collective-permute-start | bytes 1572872 | tf_op jit(solution)/shard_map/ppermute | solution.py:48
  57.9 34.8 %collective-permute-start.12 = (bf16[4,256,256]{2,1,0:T(8,128)(2,1)S(1)}, bf16[4,256,256]{2,1,0:T(8,128)(2,1)S(1)}, u32[]{:S(2)}, u32[]{:S(2)}) collective-permute-start(bf16[4,256,256]{2,1,0:T(8,128)(2,1)S(1)} %collective-permute-done.9.refs_0_), channel_id=1, source_target_pairs={{0,4},{1,5},{2,6},{3,7},{4,8},{5,9},{6,10},{7,11},{8,12},{9,13},{1... | collective-permute-start | bytes 1572872 | tf_op jit(solution)/shard_map/ppermute | solution.py:48
  58.4 34.3 %collective-permute-start.13 = (bf16[4,256,256]{2,1,0:T(8,128)(2,1)S(1)}, bf16[4,256,256]{2,1,0:T(8,128)(2,1)S(1)}, u32[]{:S(2)}, u32[]{:S(2)}) collective-permute-start(bf16[4,256,256]{2,1,0:T(8,128)(2,1)S(1)} %collective-permute-done.10.refs_1_), channel_id=1, source_target_pairs={{0,12},{1,13},{2,14},{3,15},{4,0},{5,1},{6,2},{7,3},{8,4},{9,5},{1... | collective-permute-start | bytes 1572872 | tf_op jit(solution)/shard_map/ppermute | solution.py:48
  101.1 8.5 %collective-permute-start.16 = (bf16[4,528,256]{2,1,0:T(8,128)(2,1)S(1)}, bf16[4,528,256]{2,1,0:T(8,128)(2,1)S(1)}, u32[]{:S(2)}, u32[]{:S(2)}) collective-permute-start(bf16[4,528,256]{2,1,0:T(8,128)(2,1)S(1)} %get-tuple-element.138), channel_id=1, source_target_pairs={{0,16},{1,17},{2,18},{3,19},{4,20},{5,21},{6,22},{7,23},{8,24},{9,... | collective-permute-start | bytes 3244040 | tf_op jit(solution)/shard_map/ppermute | solution.py:48
  109.6 17.9 %copy-start = (bf16[64,4096]{1,0:T(8,128)(2,1)S(1)}, bf16[64,4096]{1,0:T(8,128)(2,1)}, u32[]{:S(2)}) copy-start(bf16[64,4096]{1,0:T(8,128)(2,1)} %gate.1) | copy-start | bytes 1572868
  110.3 14.8 %collective-permute-start.17 = (bf16[528,256]{1,0:T(8,128)(2,1)S(1)}, bf16[528,256]{1,0:T(8,128)(2,1)S(1)}, u32[]{:S(2)}, u32[]{:S(2)}) collective-permute-start(bf16[528,256]{1,0:T(8,128)(2,1)S(1)} %get-tuple-element.140), channel_id=1, source_target_pairs={{0,1},{1,0},{2,3},{3,2},{4,5},{5,4},{6,7},{7,6},{8,9},{9,8},{10,11... | collective-permute-start | bytes 811016 | tf_op jit(solution)/shard_map/ppermute | solution.py:48
  110.4 14.7 %collective-permute-start.18 = (bf16[528,256]{1,0:T(8,128)(2,1)S(1)}, bf16[528,256]{1,0:T(8,128)(2,1)S(1)}, u32[]{:S(2)}, u32[]{:S(2)}) collective-permute-start(bf16[528,256]{1,0:T(8,128)(2,1)S(1)} %get-tuple-element.141), channel_id=1, source_target_pairs={{0,34},{1,3},{2,0},{3,33},{4,38},{5,7},{6,4},{7,37},{8,42},{9,11},... | collective-permute-start | bytes 811016 | tf_op jit(solution)/shard_map/ppermute | solution.py:48
  114.8 12.7 %collective-permute-start.19 = (bf16[528,256]{1,0:T(8,128)(2,1)S(1)}, bf16[528,256]{1,0:T(8,128)(2,1)S(1)}, u32[]{:S(2)}, u32[]{:S(2)}) collective-permute-start(bf16[528,256]{1,0:T(8,128)(2,1)S(1)} %get-tuple-element.142), channel_id=1, source_target_pairs={{0,35},{1,2},{2,1},{3,32},{4,39},{5,6},{6,5},{7,36},{8,43},{9,10},... | collective-permute-start | bytes 811016 | tf_op jit(solution)/shard_map/ppermute | solution.py:48
  (3 other events, 2.0 us)

commit v2 on v1

--- a/solution.py
+++ b/solution.py
@@ -208,8 +208,7 @@
         out[t, CHUNK + low : CHUNK + low + ROWS] = piece[ROWS:]
 
 
-def attend_kernel(stage, first_tile, buffers, plan, queries, *refs):
-    first, last = stage == 0, stage == 3
+def attend_kernel(first, last, stages, pieces, width, buffers, plan, queries, *refs):
     stores, refs = refs[:buffers], list(refs[buffers:])
     if not first:
         del refs[:3]
@@ -219,6 +218,7 @@
     side = plan[4 * PER_TILE]
     bounded = plan[4 * PER_TILE + 1] == 1
     per_store = stores[0].shape[0]
+    tiles = sorted({tile for _, tile, _ in pieces})
 
     if first:
         top[...] = jnp.full(top.shape, jnp.where(bounded, 0.0, EMPTY), jnp.float32)
@@ -227,96 +227,109 @@
 
     def fetch(j, part):
         rows = slice(part * CHUNK, (part + 1) * CHUNK)
+        if buffers == 1:
+            return stores[0][j, rows]
         within = lax.rem(j, per_store)
         picked = stores[0][within, rows]
         for n in range(1, buffers):
             picked = jnp.where(j >= n * per_store, stores[n][within, rows], picked)
         return picked
 
-    row = lax.broadcasted_iota(jnp.int32, (TILE, CHUNK), 0)
-    lane = lax.broadcasted_iota(jnp.int32, (TILE, CHUNK), 1)
-
-    def gather(tile, n):
-        base = (first_tile + tile) * PER_TILE
-        at = base + STAGES[stage][0] + 4 * n
-        real = [4 * n + m < plan[base + 64 + stage] for m in range(4)]
-        picks = [jnp.where(real[m], plan[at + m], 0) for m in range(4)]
-        limits = [jnp.where(real[m], plan[at + 32 + m], NEVER) for m in range(4)]
+    def gather(tile, stage, n):
+        base = tile * PER_TILE
+        at = base + 8 * stage + width * n
+        real = [width * n + m < plan[base + 64 + stage] for m in range(width)]
+        skipped = 8 * (stage - stages[0])
+        picks = [jnp.where(real[m], plan[at + m], 0) + skipped for m in range(width)]
+        limits = [jnp.where(real[m], plan[at + 32 + m], NEVER) for m in range(width)]
         keys = jnp.concatenate([fetch(j, 0) for j in picks], axis=0)
         values = jnp.concatenate([fetch(j, 1) for j in picks], axis=0)
         return keys, values, limits
 
-    def scores_of(tile, piece, rows, keys, limits):
+    def scores_of(place, rows, parity, keys, limits):
+        block = queries[place, rows]
         scores = lax.dot_general(
-            queries[tile, rows],
-            keys,
-            (((1,), (1,)), ((), ())),
-            preferred_element_type=jnp.float32,
+            block, keys, (((1,), (1,)), ((), ())), preferred_element_type=jnp.float32
         )
         scores = scores * LOG2E
-        gap = (lane ^ (side * ROWS)) - (row & (ROWS - 1)) - (side ^ piece) * ROWS
+        row = lax.broadcasted_iota(jnp.int32, (block.shape[0], CHUNK), 0)
+        lane = lax.broadcasted_iota(jnp.int32, (block.shape[0], CHUNK), 1)
+        gap = (lane ^ (side * ROWS)) - (row & (ROWS - 1)) - (side ^ parity) * ROWS
         return [
             jnp.where(gap <= limit, scores[:, m * CHUNK : (m + 1) * CHUNK], HIDDEN)
             for m, limit in enumerate(limits)
         ]
 
-    def add(tile, rows, parts, values):
+    def add(p, rows, parts, values):
         weights = [jnp.exp2(part) for part in parts]
-        total[tile, rows] += functools.reduce(jnp.add, weights)
-        acc[tile, rows] += jnp.dot(
+        total[p, rows] += functools.reduce(jnp.add, weights)
+        acc[p, rows] += jnp.dot(
             jnp.concatenate(weights, axis=-1).astype(jnp.bfloat16),
             values,
             preferred_element_type=jnp.float32,
         )
 
-    bases = [(first_tile + tile) * PER_TILE for tile in range(2)]
-    steps = (jnp.maximum(plan[bases[0] + 64 + stage], plan[bases[1] + 64 + stage]) + 3) >> 2
-
-    @pl.when(bounded)
-    def _():
-        def step(n, carry):
-            for tile in range(2):
-                keys, values, limits = gather(tile, n)
-                for piece in range(2):
-                    rows = slice(piece * TILE, (piece + 1) * TILE)
-                    add(tile, rows, scores_of(tile, piece, rows, keys, limits), values)
-            return carry
-
-        lax.fori_loop(0, steps, step, 0)
-
-    @pl.when(jnp.logical_not(bounded))
-    def _():
-        def step(n, carry):
-            tile, piece = (n >> 1) & 1, n & 1
-            keys, values, limits = gather(tile, n >> 2)
-            rows = pl.ds(pl.multiple_of(piece * TILE, TILE), TILE)
-            parts = scores_of(tile, piece, rows, keys, limits)
-            before = top[tile, rows]
-            peak = functools.reduce(jnp.maximum, parts)
-            now = jnp.maximum(before, jnp.max(peak, axis=-1, keepdims=True))
-            fading = jnp.exp2(before - now)
-            top[tile, rows] = now
-            total[tile, rows] = total[tile, rows] * fading
-            acc[tile, rows] = acc[tile, rows] * jnp.concatenate([fading, fading], axis=-1)
-            add(tile, rows, [part - now for part in parts], values)
-            return carry
-
-        lax.fori_loop(0, 4 * steps, step, 0)
+    everything = slice(None)
+    subs = TILE // 128
+
+    def one_stage(stage):
+        counts = [plan[tile * PER_TILE + 64 + stage] for tile in tiles]
+        steps = lax.div(functools.reduce(jnp.maximum, counts) + (width - 1), width)
+
+        @pl.when(bounded)
+        def _():
+            def step(n, carry):
+                for tile in tiles:
+                    keys, values, limits = gather(tile, stage, n)
+                    for p, (place, its_tile, parity) in enumerate(pieces):
+                        if its_tile == tile:
+                            parts = scores_of(place, everything, parity, keys, limits)
+                            add(p, everything, parts, values)
+                return carry
+
+            lax.fori_loop(0, steps, step, 0)
+
+        @pl.when(jnp.logical_not(bounded))
+        def _():
+            def step(n, carry):
+                p = lax.rem(lax.div(n, subs), len(pieces))
+                place, tile, parity = pieces[0]
+                for m in range(1, len(pieces)):
+                    place = jnp.where(p == m, pieces[m][0], place)
+                    tile = jnp.where(p == m, pieces[m][1], tile)
+                    parity = jnp.where(p == m, pieces[m][2], parity)
+                rows = pl.ds(pl.multiple_of(lax.rem(n, subs) * 128, 128), 128)
+                keys, values, limits = gather(tile, stage, lax.div(n, subs * len(pieces)))
+                parts = scores_of(place, rows, parity, keys, limits)
+                before = top[p, rows]
+                peak = functools.reduce(jnp.maximum, parts)
+                now = jnp.maximum(before, jnp.max(peak, axis=-1, keepdims=True))
+                fading = jnp.exp2(before - now)
+                top[p, rows] = now
+                total[p, rows] = total[p, rows] * fading
+                acc[p, rows] = acc[p, rows] * jnp.concatenate([fading, fading], axis=-1)
+                add(p, rows, [part - now for part in parts], values)
+                return carry
+
+            lax.fori_loop(0, subs * len(pieces) * steps, step, 0)
+
+    if len(stages) == 1:
+        one_stage(stages[0])
+    else:
+        lax.fori_loop(stages[0], stages[-1] + 1, lambda stage, carry: one_stage(stage) or carry, 0)
 
     if last:
-        for tile in range(2):
-            for piece in range(2):
-                logs = []
-                for sub in range(TILE // 128):
-                    rows = slice(piece * TILE + sub * 128, piece * TILE + (sub + 1) * 128)
-                    sums = jnp.sum(total[tile, rows], axis=-1, keepdims=True)
-                    some = sums > 0.0
-                    sums = jnp.where(some, sums, 1.0)
-                    result = (acc[tile, rows] / sums).astype(jnp.bfloat16)
-                    out[2 * tile + piece, sub * 128 : (sub + 1) * 128] = result
-                    level = jnp.where(some, top[tile, rows] + jnp.log2(sums), EMPTY)
-                    logs.append(level.T[:1])
-                out[2 * tile + piece, TILE:] = packed(logs)
+        for p in range(len(pieces)):
+            logs = []
+            for sub in range(TILE // 128):
+                rows = slice(sub * 128, (sub + 1) * 128)
+                sums = jnp.sum(total[p, rows], axis=-1, keepdims=True)
+                some = sums > 0.0
+                sums = jnp.where(some, sums, 1.0)
+                out[p, rows] = (acc[p, rows] / sums).astype(jnp.bfloat16)
+                level = jnp.where(some, top[p, rows] + jnp.log2(sums), EMPTY)
+                logs.append(level.T[:1])
+            out[p, TILE:] = packed(logs)
 
 
 def packed(logs):
@@ -333,12 +346,12 @@
     return rows[0:4] + rows[4:8] + rows[8:12]
 
 
-def blend(left, right):
-    a, b = unpacked(left), unpacked(right)
-    peak = jnp.maximum(a, b)
-    a, b = jnp.exp2(a - peak), jnp.exp2(b - peak)
-    both = a + b
-    return a / both, b / both, peak + jnp.log2(both)
+def blend(*parts):
+    levels = [unpacked(part) for part in parts]
+    peak = functools.reduce(jnp.maximum, levels)
+    shares = [jnp.exp2(level - peak) for level in levels]
+    whole = functools.reduce(jnp.add, shares)
+    return [share / whole for share in shares], peak + jnp.log2(whole)
 
 
 def column(shares, n):
@@ -346,27 +359,29 @@
     return jnp.concatenate([share, share], axis=-1)
 
 
+def blended(parts, shares, n):
+    rows = slice(n * 128, (n + 1) * 128)
+    return functools.reduce(
+        jnp.add,
+        [part[rows].astype(jnp.float32) * column(share, n) for part, share in zip(parts, shares)],
+    )
+
+
 def join_kernel(mine, theirs, *outs):
     for r, out in enumerate(outs):
-        a, b, level = blend(mine[r, TILE:], theirs[r, TILE:])
+        parts = (mine.at[r], theirs.at[r])
+        shares, level = blend(*[part[TILE:] for part in parts])
         for n in range(TILE // 128):
-            rows = slice(n * 128, (n + 1) * 128)
-            left = mine[r, rows].astype(jnp.float32) * column(a, n)
-            right = theirs[r, rows].astype(jnp.float32) * column(b, n)
-            out[rows] = (left + right).astype(jnp.bfloat16)
+            out[n * 128 : (n + 1) * 128] = blended(parts, shares, n).astype(jnp.bfloat16)
         out[TILE:] = packed([level])
 
 
-def finish_kernel(place, near0, near1, far0, far1, gate, out):
+def finish_kernel(place, mine, theirs, mate, far, beyond, gate, out):
     side = place[4] & 1
-    for which, (left_ref, right_ref) in enumerate(((near0, far0), (near1, far1))):
-        head = side if which == 0 else 1 - side
-        a, b, _ = blend(left_ref[TILE:], right_ref[TILE:])
+    for head, parts in ((1 - side, (mate, beyond)), (side, (far, mine, theirs))):
+        shares, _ = blend(*[part[TILE:] for part in parts])
         for n in range(TILE // 128):
-            rows = slice(n * 128, (n + 1) * 128)
-            left = left_ref[rows].astype(jnp.float32) * column(a, n)
-            right = right_ref[rows].astype(jnp.float32) * column(b, n)
-            attended = (left + right).astype(jnp.bfloat16).astype(jnp.float32)
+            attended = blended(parts, shares, n).astype(jnp.bfloat16).astype(jnp.float32)
             for m in range(2):
                 at = (head * GROUP + 2 * n + m) * DIM
                 columns = pl.ds(pl.multiple_of(at, DIM), DIM)
@@ -380,28 +395,43 @@
 BIG = pltpu.CompilerParams(vmem_limit_bytes=28 * 1024 * 1024)
 
 
-def attend(plan, queries, stores, state, stage, first_tile):
-    shapes = [
-        jax.ShapeDtypeStruct((2, 2 * TILE, width), jnp.float32) for width in (128, 128, DIM)
-    ]
-    if stage == 3:
-        shapes = [jax.ShapeDtypeStruct((4, TILE + STATS, DIM), jnp.bfloat16)] + shapes
+def attend(plan, queries, stores, state, stages, pieces, last, width=4, weight=1.0):
+    count = len(pieces)
+    shapes = [jax.ShapeDtypeStruct((count, TILE, width), jnp.float32) for width in (128, 128, DIM)]
+    if last:
+        shapes = [jax.ShapeDtypeStruct((count, TILE + STATS, DIM), jnp.bfloat16)] + shapes
     given = 2 + len(stores)
-    aliases = {given + n: n + (stage == 3) for n in range(len(state))}
-    chunks = STAGES[stage][1]
-    return pl.pallas_call(
-        functools.partial(attend_kernel, stage, first_tile, len(stores)),
+    chunks = 8 * len(stages)
+    outs = pl.pallas_call(
+        functools.partial(attend_kernel, not state, last, stages, pieces, width, len(stores)),
         in_specs=[SMEM] + [VMEM] * (1 + len(stores) + len(state)),
         out_specs=[VMEM] * len(shapes),
         out_shape=shapes,
-        input_output_aliases=aliases,
+        input_output_aliases={given + n: n + last for n in range(len(state))},
         compiler_params=BIG,
         cost_estimate=pl.CostEstimate(
-            flops=4 * 4 * TILE * chunks * CHUNK * DIM,
-            bytes_accessed=4 << 20,
-            transcendentals=4 * TILE * chunks * CHUNK,
+            flops=int(4 * count * TILE * chunks * CHUNK * DIM * weight),
+            bytes_accessed=int((4 << 20) * weight),
+            transcendentals=int(count * TILE * chunks * CHUNK * weight),
         ),
     )(plan, queries, *stores, *state)
+    return outs[0] if last else outs
+
+
+def join(mine, theirs):
+    joint = jax.ShapeDtypeStruct((TILE + STATS, DIM), jnp.bfloat16)
+    return pl.pallas_call(
+        join_kernel,
+        in_specs=[VMEM] * 2,
+        out_specs=[VMEM] * mine.shape[0],
+        out_shape=[joint] * mine.shape[0],
+        compiler_params=BIG,
+    )(mine, theirs)
+
+
+AWAY_MINE = ((1, 0, 1), (2, 1, 0), (3, 1, 1))
+AWAY_THEIRS = ((1, 2, 1), (2, 3, 0), (3, 3, 1))
+OWN = ((0, 0, 0), (1, 2, 0))
 
 
 def local(queries, gate, keys, values, q_gain, k_gain, span_of):
@@ -460,45 +490,52 @@
 
     q_mine = jnp.stack(
         [q_own, send(q_other, to_mate), send(q_own, along_z(2)), send(q_other, along_z(-1))]
-    ).reshape(2, 2 * TILE, DIM)
+    )
     low, high, q_mine = lax.optimization_barrier((low, high, q_mine))
     q_theirs = send(q_mine, to_core)
     first = [send(low, to_ring(1, 1)), send(high, to_ring(3, 1))]
-    mine = attend(plan, q_mine, [low, high], [], 0, 0)
+    mine = attend(plan, q_mine, [low, high], [], (0,), AWAY_MINE, False)
     low, high, mine = lax.optimization_barrier((low, high, mine))
     second = [send(high, to_ring(1, 1)), send(low, to_ring(3, 1))]
-    theirs = attend(plan, q_theirs, [low, high], [], 0, 2)
+    theirs = attend(plan, q_theirs, [low, high], [], (0,), AWAY_THEIRS, False)
 
     first, mine, theirs = lax.optimization_barrier((first, mine, theirs))
     last = [send(first[0], to_ring(1, 1)), send(first[1], to_ring(3, 1))]
-    mine = attend(plan, q_mine, first, mine, 1, 0)
-    theirs = attend(plan, q_theirs, first, theirs, 1, 2)
+    mine = attend(plan, q_mine, first, mine, (1,), AWAY_MINE, False)
+    theirs = attend(plan, q_theirs, first, theirs, (1,), AWAY_THEIRS, False)
     second, mine, theirs = lax.optimization_barrier((second, mine, theirs))
-    mine = attend(plan, q_mine, second, mine, 2, 0)
-    theirs = attend(plan, q_theirs, second, theirs, 2, 2)
+    mine = attend(plan, q_mine, second, mine, (2,), AWAY_MINE, False)
+    theirs = attend(plan, q_theirs, second, theirs, (2,), AWAY_THEIRS, False)
     last, mine, theirs = lax.optimization_barrier((last, mine, theirs))
-    out_theirs = attend(plan, q_theirs, last, theirs, 3, 2)[0]
+    out_theirs = attend(plan, q_theirs, last, theirs, (3,), AWAY_THEIRS, True)
     received = send(out_theirs, to_core)
-    out_mine = attend(plan, q_mine, last, mine, 3, 0)[0]
-
-    joint = jax.ShapeDtypeStruct((TILE + STATS, DIM), jnp.bfloat16)
-    parts = pl.pallas_call(
-        join_kernel,
-        in_specs=[VMEM] * 2,
-        out_specs=[VMEM] * 4,
-        out_shape=[joint] * 4,
-        compiler_params=BIG,
-    )(out_mine, received)
+    out_mine = attend(plan, q_mine, last, mine, (3,), AWAY_MINE, True)
+    parts = join(out_mine, received)
     home = [
-        parts[0],
-        send(parts[1], to_mate),
-        send(parts[2], along_z(-2)),
-        send(parts[3], along_z(-1)),
+        send(parts[0], to_mate),
+        send(parts[1], along_z(-2)),
+        send(parts[2], along_z(-1)),
     ]
+
+    stores, q_mine, q_theirs, _ = lax.optimization_barrier(
+        ([low, high] + first + second + last, q_mine, q_theirs, parts)
+    )
+    out = attend(
+        plan,
+        jnp.stack([q_mine[0], q_theirs[0]]),
+        [jnp.concatenate(stores, axis=0)],
+        [],
+        (0, 1, 2, 3),
+        OWN,
+        True,
+        8,
+        0.01,
+    )
+    home = [out[0], send(out[1], to_core), *home]
 
     return pl.pallas_call(
         finish_kernel,
-        in_specs=[SMEM] + [VMEM] * 5,
+        in_specs=[SMEM] + [VMEM] * 6,
         out_specs=VMEM,
         out_shape=jax.ShapeDtypeStruct(queries.shape, jnp.bfloat16),
         compiler_params=BIG,

time: 130 us -> 179 us (1.38)
  the two profiles are of different devices: /device:TPU:4 before, /device:TPU:1 now
where the time goes in v2:
time: 179 us; the launch traced here: 178 us
  Pallas kernels  130 us (73%)
  starting transfers between devices  34.6 us (19%)
  waiting for transfers between devices  8.38 us (5%)
  local copies, waits for them, and re-layouts  5.19 us (3%)
    pallas_call x9, Pallas kernels, attend(): pl.pallas_call(functools.partial(attend_kernel, not state, last, stages,...  122 us
    ppermute x21, starting transfers between devices, send(): return lax.ppermute(array, AXES, route)  34.6 us
    ppermute x21, waiting for transfers between devices, send(): return lax.ppermute(array, AXES, route)  8.38 us
    unnamed x21, local copies, waits for them, and re-layouts  5 us
    pallas_call x1, Pallas kernels, local(): pl.pallas_call(prepare_kernel, in_specs=[SMEM] * 2 + [VMEM] * 3 + [pl.Blo...  3.96 us
  transfers between devices with their start and end apart: 21, of which 2 were waited for; matrix products, arithmetic and copies ran while one was open for 0% of the time, Pallas kernels for 64%

profile of v2, /device:TPU:1, one launch (start us, length us, event | category | flops | bytes accessed | tf_op | source)
XLA Modules:
  0.0 178.4 jit_solution(2415133869411688772)
XLA Ops:
  2.4 7.4 %collective-permute-start.2 = (bf16[128,256]{1,0:T(8,128)(2,1)S(1)}, bf16[128,256]{1,0:T(8,128)(2,1)S(1)}, u32[]{:S(2)}, u32[]{:S(2)}) collective-permute-start(bf16[128,256]{1,0:T(8,128)(2,1)S(1)} %get-tuple-element.87), channel_id=1, source_target_pairs={{0,33},{1,32},{2,35},{3,34},{4,37},{5,36},{6,39},{7,38},{8,41},{9,... | collective-permute-start | bytes 196616 | tf_op jit(solution)/shard_map/ppermute | solution.py:48
  14.1 4.0 %shard_map.74 = (s32[296]{0:T(512)S(1)}, f32[256,128]{1,0:T(8,128)S(1)}, f32[256,128]{1,0:T(8,128)S(1)}, bf16[512,256]{1,0:T(8,128)(2,1)S(1)}, bf16[512,256]{1,0:T(8,128)(2,1)S(1)}) custom-call(s32[5]{0:T(128)S(1)} %stack.41.place, s32[32]{0:T(128)S(1)} %copy-done.6, f32[1,128]{1,0:T(1,128)S(1)} %fusion.2.frequency, f32[1,256]{1,0:T(1,128)S(1)} %bitcast.18, ...), custom_call_target="tpu_custom_call" | custom-call | tf_op jit(solution)/shard_map/pallas_call | solution.py:460
  18.4 1.4 collective-permute-start.3
  19.8 1.2 collective-permute-start.7
  21.0 3.5 %collective-permute-start.8 = (bf16[512,256]{1,0:T(8,128)(2,1)S(1)}, bf16[512,256]{1,0:T(8,128)(2,1)S(1)}, u32[]{:S(2)}, u32[]{:S(2)}) collective-permute-start(bf16[512,256]{1,0:T(8,128)(2,1)S(1)} %get-tuple-element.96), channel_id=1, source_target_pairs={{0,35},{1,2},{2,1},{3,32},{4,39},{5,6},{6,5},{7,36},{8,43},{9,10},... | collective-permute-start | bytes 786440 | tf_op jit(solution)/shard_map/ppermute | solution.py:48
  25.2 2.6 %collective-permute-start.5 = (bf16[2,256,256]{2,1,0:T(8,128)(2,1)S(1)}, bf16[2,256,256]{2,1,0:T(8,128)(2,1)S(1)}, u32[]{:S(2)}, u32[]{:S(2)}) collective-permute-start(bf16[2,256,256]{2,1,0:T(8,128)(2,1)S(1)} %shard_map.75), channel_id=1, source_target_pairs={{0,128},{1,129},{2,130},{3,131},{4,132},{5,133},{6,134},{7,135},{8... | collective-permute-start | bytes 786440 | tf_op jit(solution)/shard_map/ppermute | solution.py:48
  29.0 7.2 %collective-permute-done.8 = bf16[512,256]{1,0:T(8,128)(2,1)S(1)} collective-permute-done((bf16[512,256]{1,0:T(8,128)(2,1)S(1)}, bf16[512,256]{1,0:T(8,128)(2,1)S(1)}, u32[]{:S(2)}, u32[]{:S(2)}) %collective-permute-start.8) | collective-permute-done | bytes 262176 | tf_op jit(solution)/shard_map/ppermute | solution.py:48
  36.4 1.4 collective-permute-start.11
  37.7 1.7 collective-permute-start.9
  40.4 12.3 %shard_map.76 = (f32[3,512,128]{2,1,0:T(8,128)S(1)}, f32[3,512,128]{2,1,0:T(8,128)S(1)}, f32[3,512,256]{2,1,0:T(8,128)S(1)}) custom-call(s32[296]{0:T(512)S(1)} %get-tuple-element.86.plan, bf16[4,512,256]{2,1,0:T(8,128)(2,1)S(1)} %pad_maximum_fusion.queries, bf16[4,256,256]{2,1,0:T(8,128)(2,1)S(1)} %pad_maximum_fusion.1.refs_0_, ...), custom_call_target="tpu_custom_call" | custom-call | flops 1610612736 | bytes 4194304 | tf_op jit(solution)/shard_map/pallas_call | solution.py:405
  52.6 1.5 collective-permute-start.13
  54.4 12.3 %shard_map.77 = (f32[3,512,128]{2,1,0:T(8,128)S(1)}, f32[3,512,128]{2,1,0:T(8,128)S(1)}, f32[3,512,256]{2,1,0:T(8,128)S(1)}) custom-call(s32[296]{0:T(512)S(1)} %get-tuple-element.86.plan, bf16[4,512,256]{2,1,0:T(8,128)(2,1)S(1)} %collective-permute-done.11.queries, bf16[4,256,256]{2,1,0:T(8,128)(2,1)S(1)} %pad_maximum_fusion.1.refs_0_, ...), custom_call_target="tpu_custom_call" | custom-call | flops 1610612736 | bytes 4194304 | tf_op jit(solution)/shard_map/pallas_call | solution.py:405
  66.8 2.7 %collective-permute-start.15 = (bf16[4,256,256]{2,1,0:T(8,128)(2,1)S(1)}, bf16[4,256,256]{2,1,0:T(8,128)(2,1)S(1)}, u32[]{:S(2)}, u32[]{:S(2)}) collective-permute-start(bf16[4,256,256]{2,1,0:T(8,128)(2,1)S(1)} %collective-permute-done.10.refs_1_), channel_id=1, source_target_pairs={{0,12},{1,13},{2,14},{3,15},{4,0},{5,1},{6,2},{7,3},{8,4},{9,5},{1... | collective-permute-start | bytes 1572872 | tf_op jit(solution)/shard_map/ppermute | solution.py:48
  69.4 12.0 %shard_map.78 = (f32[3,512,128]{2,1,0:T(8,128)S(1)}, f32[3,512,128]{2,1,0:T(8,128)S(1)}, f32[3,512,256]{2,1,0:T(8,128)S(1)}) custom-call(s32[296]{0:T(512)S(1)} %get-tuple-element.86.plan, bf16[4,512,256]{2,1,0:T(8,128)(2,1)S(1)} %pad_maximum_fusion.queries, ...), custom_call_target="tpu_custom_call", output_to_operand_aliasing={{0}: (4, {}), {1}: (5, {}), {2}: (6, {})} | custom-call | flops 1610612736 | bytes 4194304 | tf_op jit(solution)/shard_map/pallas_call | solution.py:405
  81.5 12.0 %shard_map.79 = (f32[3,512,128]{2,1,0:T(8,128)S(1)}, f32[3,512,128]{2,1,0:T(8,128)S(1)}, f32[3,512,256]{2,1,0:T(8,128)S(1)}) custom-call(s32[296]{0:T(512)S(1)} %get-tuple-element.86.plan, bf16[4,512,256]{2,1,0:T(8,128)(2,1)S(1)} %collective-permute-done.11.queries, ...), custom_call_target="tpu_custom_call", output_to_operand_aliasing={{0}: (4, {}), {1}: (5, {}), {2}: (6, {})} | custom-call | flops 1610612736 | bytes 4194304 | tf_op jit(solution)/shard_map/pallas_call | solution.py:405
  93.5 12.1 %shard_map.80 = (f32[3,512,128]{2,1,0:T(8,128)S(1)}, f32[3,512,128]{2,1,0:T(8,128)S(1)}, f32[3,512,256]{2,1,0:T(8,128)S(1)}) custom-call(s32[296]{0:T(512)S(1)} %get-tuple-element.86.plan, bf16[4,512,256]{2,1,0:T(8,128)(2,1)S(1)} %pad_maximum_fusion.queries, ...), custom_call_target="tpu_custom_call", output_to_operand_aliasing={{0}: (4, {}), {1}: (5, {}), {2}: (6, {})} | custom-call | flops 1610612736 | bytes 4194304 | tf_op jit(solution)/shard_map/pallas_call | solution.py:405
  105.6 12.0 %shard_map.81 = (f32[3,512,128]{2,1,0:T(8,128)S(1)}, f32[3,512,128]{2,1,0:T(8,128)S(1)}, f32[3,512,256]{2,1,0:T(8,128)S(1)}) custom-call(s32[296]{0:T(512)S(1)} %get-tuple-element.86.plan, bf16[4,512,256]{2,1,0:T(8,128)(2,1)S(1)} %collective-permute-done.11.queries, ...), custom_call_target="tpu_custom_call", output_to_operand_aliasing={{0}: (4, {}), {1}: (5, {}), {2}: (6, {})} | custom-call | flops 1610612736 | bytes 4194304 | tf_op jit(solution)/shard_map/pallas_call | solution.py:405
  117.6 12.5 %shard_map.83 = (bf16[3,528,256]{2,1,0:T(8,128)(2,1)S(1)}, f32[3,512,128]{2,1,0:T(8,128)S(1)}, f32[3,512,128]{2,1,0:T(8,128)S(1)}, f32[3,512,256]{2,1,0:T(8,128)S(1)}) custom-call(s32[296]{0:T(512)S(1)} %get-tuple-element.86.plan, ...), custom_call_target="tpu_custom_call", output_to_operand_aliasing={{1}: (4, {}), {2}: (5, {}), {3}: (6, {})} | custom-call | flops 1610612736 | bytes 4194304 | tf_op jit(solution)/shard_map/pallas_call | solution.py:405
  130.1 2.1 %collective-permute-start.16 = (bf16[3,528,256]{2,1,0:T(8,128)(2,1)S(1)}, bf16[3,528,256]{2,1,0:T(8,128)(2,1)S(1)}, u32[]{:S(2)}, u32[]{:S(2)}) collective-permute-start(bf16[3,528,256]{2,1,0:T(8,128)(2,1)S(1)} %get-tuple-element.148), channel_id=1, source_target_pairs={{0,16},{1,17},{2,18},{3,19},{4,20},{5,21},{6,22},{7,23},{8,24},{9,... | collective-permute-start | bytes 2433032 | tf_op jit(solution)/shard_map/ppermute | solution.py:48
  132.2 12.6 %shard_map.82 = (bf16[3,528,256]{2,1,0:T(8,128)(2,1)S(1)}, f32[3,512,128]{2,1,0:T(8,128)S(1)}, f32[3,512,128]{2,1,0:T(8,128)S(1)}, f32[3,512,256]{2,1,0:T(8,128)S(1)}) custom-call(s32[296]{0:T(512)S(1)} %get-tuple-element.86.plan, bf16[4,512,256]{2,1,0:T(8,128)(2,1)S(1)} %pad_maximum_fusion.queries, ...), custom_call_target="tpu_custom_call", output_to_operand_aliasing={{1}: (4, {}), {2}: (5, {}), {3}: (6, {})} | custom-call | flops 1610612736 | bytes 4194304 | tf_op jit(solution)/shard_map/pallas_call | solution.py:405
  145.4 3.5 %collective-permute-start.19 = (bf16[528,256]{1,0:T(8,128)(2,1)S(1)}, bf16[528,256]{1,0:T(8,128)(2,1)S(1)}, u32[]{:S(2)}, u32[]{:S(2)}) collective-permute-start(bf16[528,256]{1,0:T(8,128)(2,1)S(1)} %get-tuple-element.150), channel_id=1, source_target_pairs={{0,34},{1,3},{2,0},{3,33},{4,38},{5,7},{6,4},{7,37},{8,42},{9,11},... | collective-permute-start | bytes 811016 | tf_op jit(solution)/shard_map/ppermute | solution.py:48
  149.7 24.8 %shard_map.85 = (bf16[2,528,256]{2,1,0:T(8,128)(2,1)S(1)}, f32[2,512,128]{2,1,0:T(8,128)}, f32[2,512,128]{2,1,0:T(8,128)}, f32[2,512,256]{2,1,0:T(8,128)}) custom-call(s32[296]{0:T(512)S(1)} %get-tuple-element.86.plan, bf16[2,512,256]{2,1,0:T(8,128)(2,1)S(1)} %pad_maximum_fusion.3.queries, bf16[32,256,256]{2,1,0:T(8,128)(2,1)S(1)} %constant_dynamic-update-slice_fusion.refs_0_), custom_call_target="tpu_custom_call" | custom-call | flops 42949672 | bytes 41943 | tf_op jit(solution)/shard_map/pallas_call | solution.py:405
  175.4 1.2 collective-permute-done.17.theirs
  176.6 1.9 %shard_map.86 = bf16[64,4096]{1,0:T(8,128)(2,1)} custom-call(s32[5]{0:T(128)S(1)} %stack.41.place, bf16[528,256]{1,0:T(8,128)(2,1)S(1)} %get-tuple-element.164.mine, bf16[528,256]{1,0:T(8,128)(2,1)S(1)} %collective-permute-done.17.theirs, bf16[528,256]{1,0:T(8,128)(2,1)S(1)} %collective-permute-done.18.mate, ...), custom_call_target="tpu_custom_call" | custom-call | tf_op jit(solution)/shard_map/pallas_call | solution.py:536
  (63 shorter events, 12.7 us)
Async XLA Ops:
  0.1 0.8 copy-start.2
  2.4 15.7 %collective-permute-start.2 = (bf16[128,256]{1,0:T(8,128)(2,1)S(1)}, bf16[128,256]{1,0:T(8,128)(2,1)S(1)}, u32[]{:S(2)}, u32[]{:S(2)}) collective-permute-start(bf16[128,256]{1,0:T(8,128)(2,1)S(1)} %get-tuple-element.87), channel_id=1, source_target_pairs={{0,33},{1,32},{2,35},{3,34},{4,37},{5,36},{6,39},{7,38},{8,41},{9,... | collective-permute-start | bytes 196616 | tf_op jit(solution)/shard_map/ppermute | solution.py:48
  9.8 8.3 %collective-permute-start = (bf16[128,256]{1,0:T(8,128)(2,1)S(1)}, bf16[128,256]{1,0:T(8,128)(2,1)S(1)}, u32[]{:S(2)}, u32[]{:S(2)}) collective-permute-start(bf16[128,256]{1,0:T(8,128)(2,1)S(1)} %get-tuple-element.87), channel_id=1, source_target_pairs={{0,1},{1,0},{2,3},{3,2},{4,5},{5,4},{6,7},{7,6},{8,9},{9,8},{10,11... | collective-permute-start | bytes 196616 | tf_op jit(solution)/shard_map/ppermute | solution.py:48
  10.5 7.6 %collective-permute-start.1 = (bf16[128,256]{1,0:T(8,128)(2,1)S(1)}, bf16[128,256]{1,0:T(8,128)(2,1)S(1)}, u32[]{:S(2)}, u32[]{:S(2)}) collective-permute-start(bf16[128,256]{1,0:T(8,128)(2,1)S(1)} %get-tuple-element.84.own), channel_id=1, source_target_pairs={{0,32},{1,33},{2,34},{3,35},{4,36},{5,37},{6,38},{7,39},{8,40},{9,... | collective-permute-start | bytes 196616 | tf_op jit(solution)/shard_map/ppermute | solution.py:48
  11.1 1.0 copy-start
  18.4 9.4 %collective-permute-start.3 = (bf16[2,256,256]{2,1,0:T(8,128)(2,1)S(1)}, bf16[2,256,256]{2,1,0:T(8,128)(2,1)S(1)}, u32[]{:S(2)}, u32[]{:S(2)}) collective-permute-start(bf16[2,256,256]{2,1,0:T(8,128)(2,1)S(1)} %shard_map.75), channel_id=1, source_target_pairs={{0,64},{1,65},{2,66},{3,67},{4,68},{5,69},{6,70},{7,71},{8,72},{9,... | collective-permute-start | bytes 786440 | tf_op jit(solution)/shard_map/ppermute | solution.py:48
  19.8 9.1 %collective-permute-start.7 = (bf16[512,256]{1,0:T(8,128)(2,1)S(1)}, bf16[512,256]{1,0:T(8,128)(2,1)S(1)}, u32[]{:S(2)}, u32[]{:S(2)}) collective-permute-start(bf16[512,256]{1,0:T(8,128)(2,1)S(1)} %get-tuple-element.95), channel_id=1, source_target_pairs={{0,2},{1,35},{2,32},{3,1},{4,6},{5,39},{6,36},{7,5},{8,10},{9,43},... | collective-permute-start | bytes 786440 | tf_op jit(solution)/shard_map/ppermute | solution.py:48
  21.0 15.1 %collective-permute-start.8 = (bf16[512,256]{1,0:T(8,128)(2,1)S(1)}, bf16[512,256]{1,0:T(8,128)(2,1)S(1)}, u32[]{:S(2)}, u32[]{:S(2)}) collective-permute-start(bf16[512,256]{1,0:T(8,128)(2,1)S(1)} %get-tuple-element.96), channel_id=1, source_target_pairs={{0,35},{1,2},{2,1},{3,32},{4,39},{5,6},{6,5},{7,36},{8,43},{9,10},... | collective-permute-start | bytes 786440 | tf_op jit(solution)/shard_map/ppermute | solution.py:48
  24.5 11.7 %collective-permute-start.6 = (bf16[512,256]{1,0:T(8,128)(2,1)S(1)}, bf16[512,256]{1,0:T(8,128)(2,1)S(1)}, u32[]{:S(2)}, u32[]{:S(2)}) collective-permute-start(bf16[512,256]{1,0:T(8,128)(2,1)S(1)} %get-tuple-element.96), channel_id=1, source_target_pairs={{0,1},{1,0},{2,3},{3,2},{4,5},{5,4},{6,7},{7,6},{8,9},{9,8},{10,11... | collective-permute-start | bytes 786440 | tf_op jit(solution)/shard_map/ppermute | solution.py:48
  25.2 11.1 %collective-permute-start.5 = (bf16[2,256,256]{2,1,0:T(8,128)(2,1)S(1)}, bf16[2,256,256]{2,1,0:T(8,128)(2,1)S(1)}, u32[]{:S(2)}, u32[]{:S(2)}) collective-permute-start(bf16[2,256,256]{2,1,0:T(8,128)(2,1)S(1)} %shard_map.75), channel_id=1, source_target_pairs={{0,128},{1,129},{2,130},{3,131},{4,132},{5,133},{6,134},{7,135},{8... | collective-permute-start | bytes 786440 | tf_op jit(solution)/shard_map/ppermute | solution.py:48
  27.8 8.5 %collective-permute-start.4 = (bf16[2,256,256]{2,1,0:T(8,128)(2,1)S(1)}, bf16[2,256,256]{2,1,0:T(8,128)(2,1)S(1)}, u32[]{:S(2)}, u32[]{:S(2)}) collective-permute-start(bf16[2,256,256]{2,1,0:T(8,128)(2,1)S(1)} %shard_map.75), channel_id=1, source_target_pairs={{0,192},{1,193},{2,194},{3,195},{4,196},{5,197},{6,198},{7,199},{8... | collective-permute-start | bytes 786440 | tf_op jit(solution)/shard_map/ppermute | solution.py:48
  36.4 18.0 %collective-permute-start.11 = (bf16[4,512,256]{2,1,0:T(8,128)(2,1)S(1)}, bf16[4,512,256]{2,1,0:T(8,128)(2,1)S(1)}, u32[]{:S(2)}, u32[]{:S(2)}) collective-permute-start(bf16[4,512,256]{2,1,0:T(8,128)(2,1)S(1)} %pad_maximum_fusion.queries), channel_id=1, source_target_pairs={{0,16},{1,17},{2,18},{3,19},{4,20},{5,21},{6,22},{7,23},{8,24},{9,... | collective-permute-start | bytes 3145736 | tf_op jit(solution)/shard_map/ppermute | solution.py:48
  37.7 29.0 %collective-permute-start.9 = (bf16[4,256,256]{2,1,0:T(8,128)(2,1)S(1)}, bf16[4,256,256]{2,1,0:T(8,128)(2,1)S(1)}, u32[]{:S(2)}, u32[]{:S(2)}) collective-permute-start(bf16[4,256,256]{2,1,0:T(8,128)(2,1)S(1)} %pad_maximum_fusion.1.refs_0_), channel_id=1, source_target_pairs={{0,4},{1,5},{2,6},{3,7},{4,8},{5,9},{6,10},{7,11},{8,12},{9,13},{1... | collective-permute-start | bytes 1572872 | tf_op jit(solution)/shard_map/ppermute | solution.py:48
  39.4 27.3 %collective-permute-start.10 = (bf16[4,256,256]{2,1,0:T(8,128)(2,1)S(1)}, bf16[4,256,256]{2,1,0:T(8,128)(2,1)S(1)}, u32[]{:S(2)}, u32[]{:S(2)}) collective-permute-start(bf16[4,256,256]{2,1,0:T(8,128)(2,1)S(1)} %pad_maximum_fusion.2.refs_1_), channel_id=1, source_target_pairs={{0,12},{1,13},{2,14},{3,15},{4,0},{5,1},{6,2},{7,3},{8,4},{9,5},{1... | collective-permute-start | bytes 1572872 | tf_op jit(solution)/shard_map/ppermute | solution.py:48
  52.6 40.9 %collective-permute-start.13 = (bf16[4,256,256]{2,1,0:T(8,128)(2,1)S(1)}, bf16[4,256,256]{2,1,0:T(8,128)(2,1)S(1)}, u32[]{:S(2)}, u32[]{:S(2)}) collective-permute-start(bf16[4,256,256]{2,1,0:T(8,128)(2,1)S(1)} %pad_maximum_fusion.1.refs_0_), channel_id=1, source_target_pairs={{0,12},{1,13},{2,14},{3,15},{4,0},{5,1},{6,2},{7,3},{8,4},{9,5},{1... | collective-permute-start | bytes 1572872 | tf_op jit(solution)/shard_map/ppermute | solution.py:48
  54.2 39.3 %collective-permute-start.12 = (bf16[4,256,256]{2,1,0:T(8,128)(2,1)S(1)}, bf16[4,256,256]{2,1,0:T(8,128)(2,1)S(1)}, u32[]{:S(2)}, u32[]{:S(2)}) collective-permute-start(bf16[4,256,256]{2,1,0:T(8,128)(2,1)S(1)} %pad_maximum_fusion.2.refs_1_), channel_id=1, source_target_pairs={{0,4},{1,5},{2,6},{3,7},{4,8},{5,9},{6,10},{7,11},{8,12},{9,13},{1... | collective-permute-start | bytes 1572872 | tf_op jit(solution)/shard_map/ppermute | solution.py:48
  66.7 50.9 %collective-permute-start.14 = (bf16[4,256,256]{2,1,0:T(8,128)(2,1)S(1)}, bf16[4,256,256]{2,1,0:T(8,128)(2,1)S(1)}, u32[]{:S(2)}, u32[]{:S(2)}) collective-permute-start(bf16[4,256,256]{2,1,0:T(8,128)(2,1)S(1)} %collective-permute-done.9.refs_0_), channel_id=1, source_target_pairs={{0,4},{1,5},{2,6},{3,7},{4,8},{5,9},{6,10},{7,11},{8,12},{9,13},{1... | collective-permute-start | bytes 1572872 | tf_op jit(solution)/shard_map/ppermute | solution.py:48
  66.8 50.8 %collective-permute-start.15 = (bf16[4,256,256]{2,1,0:T(8,128)(2,1)S(1)}, bf16[4,256,256]{2,1,0:T(8,128)(2,1)S(1)}, u32[]{:S(2)}, u32[]{:S(2)}) collective-permute-start(bf16[4,256,256]{2,1,0:T(8,128)(2,1)S(1)} %collective-permute-done.10.refs_1_), channel_id=1, source_target_pairs={{0,12},{1,13},{2,14},{3,15},{4,0},{5,1},{6,2},{7,3},{8,4},{9,5},{1... | collective-permute-start | bytes 1572872 | tf_op jit(solution)/shard_map/ppermute | solution.py:48
  130.1 14.6 %collective-permute-start.16 = (bf16[3,528,256]{2,1,0:T(8,128)(2,1)S(1)}, bf16[3,528,256]{2,1,0:T(8,128)(2,1)S(1)}, u32[]{:S(2)}, u32[]{:S(2)}) collective-permute-start(bf16[3,528,256]{2,1,0:T(8,128)(2,1)S(1)} %get-tuple-element.148), channel_id=1, source_target_pairs={{0,16},{1,17},{2,18},{3,19},{4,20},{5,21},{6,22},{7,23},{8,24},{9,... | collective-permute-start | bytes 2433032 | tf_op jit(solution)/shard_map/ppermute | solution.py:48
  145.2 30.2 %collective-permute-start.18 = (bf16[528,256]{1,0:T(8,128)(2,1)S(1)}, bf16[528,256]{1,0:T(8,128)(2,1)S(1)}, u32[]{:S(2)}, u32[]{:S(2)}) collective-permute-start(bf16[528,256]{1,0:T(8,128)(2,1)S(1)} %get-tuple-element.149), channel_id=1, source_target_pairs={{0,1},{1,0},{2,3},{3,2},{4,5},{5,4},{6,7},{7,6},{8,9},{9,8},{10,11... | collective-permute-start | bytes 811016 | tf_op jit(solution)/shard_map/ppermute | solution.py:48
  145.4 30.1 %collective-permute-start.19 = (bf16[528,256]{1,0:T(8,128)(2,1)S(1)}, bf16[528,256]{1,0:T(8,128)(2,1)S(1)}, u32[]{:S(2)}, u32[]{:S(2)}) collective-permute-start(bf16[528,256]{1,0:T(8,128)(2,1)S(1)} %get-tuple-element.150), channel_id=1, source_target_pairs={{0,34},{1,3},{2,0},{3,33},{4,38},{5,7},{6,4},{7,37},{8,42},{9,11},... | collective-permute-start | bytes 811016 | tf_op jit(solution)/shard_map/ppermute | solution.py:48
  148.9 26.5 %collective-permute-start.20 = (bf16[528,256]{1,0:T(8,128)(2,1)S(1)}, bf16[528,256]{1,0:T(8,128)(2,1)S(1)}, u32[]{:S(2)}, u32[]{:S(2)}) collective-permute-start(bf16[528,256]{1,0:T(8,128)(2,1)S(1)} %get-tuple-element.151), channel_id=1, source_target_pairs={{0,35},{1,2},{2,1},{3,32},{4,39},{5,6},{6,5},{7,36},{8,43},{9,10},... | collective-permute-start | bytes 811016 | tf_op jit(solution)/shard_map/ppermute | solution.py:48
  149.6 27.0 %copy-start.1 = (bf16[64,4096]{1,0:T(8,128)(2,1)S(1)}, bf16[64,4096]{1,0:T(8,128)(2,1)}, u32[]{:S(2)}) copy-start(bf16[64,4096]{1,0:T(8,128)(2,1)} %gate.1) | copy-start | bytes 1572868
  174.5 2.1 %collective-permute-start.17 = (bf16[528,256]{1,0:T(8,128)(2,1)S(1)}, bf16[528,256]{1,0:T(8,128)(2,1)S(1)}, u32[]{:S(2)}, u32[]{:S(2)}) collective-permute-start(bf16[528,256]{1,0:T(8,128)(2,1)S(1)} %get-tuple-element.163), channel_id=1, source_target_pairs={{0,16},{1,17},{2,18},{3,19},{4,20},{5,21},{6,22},{7,23},{8,24},{9,... | collective-permute-start | bytes 811016 | tf_op jit(solution)/shard_map/ppermute | solution.py:48
  (4 other events, 2.9 us)

commit v3 on v2

--- a/solution.py
+++ b/solution.py
@@ -507,9 +507,9 @@
     mine = attend(plan, q_mine, second, mine, (2,), AWAY_MINE, False)
     theirs = attend(plan, q_theirs, second, theirs, (2,), AWAY_THEIRS, False)
     last, mine, theirs = lax.optimization_barrier((last, mine, theirs))
-    out_theirs = attend(plan, q_theirs, last, theirs, (3,), AWAY_THEIRS, True)
+    out_theirs = attend(plan, q_theirs, last, theirs, (3,), AWAY_THEIRS, True, 8)
     received = send(out_theirs, to_core)
-    out_mine = attend(plan, q_mine, last, mine, (3,), AWAY_MINE, True)
+    out_mine = attend(plan, q_mine, last, mine, (3,), AWAY_MINE, True, 8)
     parts = join(out_mine, received)
     home = [
         send(parts[0], to_mate),

time: 179 us -> 173 us (0.966)
  Pallas kernels: 130 us -> 119 us
  starting transfers between devices: 34.6 us -> 38.7 us
    pallas_call x9, Pallas kernels: 122 us -> 111 us  [attend(): pl.pallas_call(functools.partial(attend_kernel, not state, last, stages,...]
    ppermute x21, starting transfers between devices: 34.6 us -> 38.7 us  [send(): return lax.ppermute(array, AXES, route)]
  transfers between devices with their start and end apart: 21 -> 21, of which waited for: 2 -> 2; matrix products, arithmetic and copies ran while one was open for 0% -> 0% of each run, Pallas kernels for 64% -> 61%
where the time goes in v3:
time: 173 us; the launch traced here: 172 us
  Pallas kernels  119 us (69%)
  starting transfers between devices  38.7 us (22%)
  waiting for transfers between devices  8.38 us (5%)
  local copies, waits for them, and re-layouts  5.19 us (3%)
    pallas_call x9, Pallas kernels, attend(): pl.pallas_call(functools.partial(attend_kernel, not state, last, stages,...  111 us
    ppermute x21, starting transfers between devices, send(): return lax.ppermute(array, AXES, route)  38.7 us
    ppermute x21, waiting for transfers between devices, send(): return lax.ppermute(array, AXES, route)  8.38 us
    unnamed x21, local copies, waits for them, and re-layouts  5 us
    pallas_call x1, Pallas kernels, local(): pl.pallas_call(prepare_kernel, in_specs=[SMEM] * 2 + [VMEM] * 3 + [pl.Blo...  3.96 us
  transfers between devices with their start and end apart: 21, of which 2 were waited for; matrix products, arithmetic and copies ran while one was open for 0% of the time, Pallas kernels for 61%

profile of v3, /device:TPU:1, one launch (start us, length us, event | category | flops | bytes accessed | tf_op | source)
XLA Modules:
  0.0 171.5 jit_solution(9062278303489649250)
XLA Ops:
  2.4 7.4 %collective-permute-start.2 = (bf16[128,256]{1,0:T(8,128)(2,1)S(1)}, bf16[128,256]{1,0:T(8,128)(2,1)S(1)}, u32[]{:S(2)}, u32[]{:S(2)}) collective-permute-start(bf16[128,256]{1,0:T(8,128)(2,1)S(1)} %get-tuple-element.87), channel_id=1, source_target_pairs={{0,33},{1,32},{2,35},{3,34},{4,37},{5,36},{6,39},{7,38},{8,41},{9,... | collective-permute-start | bytes 196616 | tf_op jit(solution)/shard_map/ppermute | solution.py:48
  14.1 4.0 %shard_map.74 = (s32[296]{0:T(512)S(1)}, f32[256,128]{1,0:T(8,128)S(1)}, f32[256,128]{1,0:T(8,128)S(1)}, bf16[512,256]{1,0:T(8,128)(2,1)S(1)}, bf16[512,256]{1,0:T(8,128)(2,1)S(1)}) custom-call(s32[5]{0:T(128)S(1)} %stack.41.place, s32[32]{0:T(128)S(1)} %copy-done.6, f32[1,128]{1,0:T(1,128)S(1)} %fusion.2.frequency, f32[1,256]{1,0:T(1,128)S(1)} %bitcast.18, ...), custom_call_target="tpu_custom_call" | custom-call | tf_op jit(solution)/shard_map/pallas_call | solution.py:460
  18.4 1.4 collective-permute-start.3
  19.8 1.2 collective-permute-start.7
  21.0 3.5 %collective-permute-start.8 = (bf16[512,256]{1,0:T(8,128)(2,1)S(1)}, bf16[512,256]{1,0:T(8,128)(2,1)S(1)}, u32[]{:S(2)}, u32[]{:S(2)}) collective-permute-start(bf16[512,256]{1,0:T(8,128)(2,1)S(1)} %get-tuple-element.96), channel_id=1, source_target_pairs={{0,35},{1,2},{2,1},{3,32},{4,39},{5,6},{6,5},{7,36},{8,43},{9,10},... | collective-permute-start | bytes 786440 | tf_op jit(solution)/shard_map/ppermute | solution.py:48
  25.2 2.6 %collective-permute-start.5 = (bf16[2,256,256]{2,1,0:T(8,128)(2,1)S(1)}, bf16[2,256,256]{2,1,0:T(8,128)(2,1)S(1)}, u32[]{:S(2)}, u32[]{:S(2)}) collective-permute-start(bf16[2,256,256]{2,1,0:T(8,128)(2,1)S(1)} %shard_map.75), channel_id=1, source_target_pairs={{0,128},{1,129},{2,130},{3,131},{4,132},{5,133},{6,134},{7,135},{8... | collective-permute-start | bytes 786440 | tf_op jit(solution)/shard_map/ppermute | solution.py:48
  29.0 7.2 %collective-permute-done.8 = bf16[512,256]{1,0:T(8,128)(2,1)S(1)} collective-permute-done((bf16[512,256]{1,0:T(8,128)(2,1)S(1)}, bf16[512,256]{1,0:T(8,128)(2,1)S(1)}, u32[]{:S(2)}, u32[]{:S(2)}) %collective-permute-start.8) | collective-permute-done | bytes 262176 | tf_op jit(solution)/shard_map/ppermute | solution.py:48
  36.4 1.4 collective-permute-start.11
  37.7 1.7 collective-permute-start.9
  40.4 12.3 %shard_map.76 = (f32[3,512,128]{2,1,0:T(8,128)S(1)}, f32[3,512,128]{2,1,0:T(8,128)S(1)}, f32[3,512,256]{2,1,0:T(8,128)S(1)}) custom-call(s32[296]{0:T(512)S(1)} %get-tuple-element.86.plan, bf16[4,512,256]{2,1,0:T(8,128)(2,1)S(1)} %pad_maximum_fusion.queries, bf16[4,256,256]{2,1,0:T(8,128)(2,1)S(1)} %pad_maximum_fusion.1.refs_0_, ...), custom_call_target="tpu_custom_call" | custom-call | flops 1610612736 | bytes 4194304 | tf_op jit(solution)/shard_map/pallas_call | solution.py:405
  52.6 1.5 collective-permute-start.13
  54.4 6.5 %shard_map.77 = (f32[3,512,128]{2,1,0:T(8,128)S(1)}, f32[3,512,128]{2,1,0:T(8,128)S(1)}, f32[3,512,256]{2,1,0:T(8,128)S(1)}) custom-call(s32[296]{0:T(512)S(1)} %get-tuple-element.86.plan, bf16[4,512,256]{2,1,0:T(8,128)(2,1)S(1)} %collective-permute-done.11.queries, bf16[4,256,256]{2,1,0:T(8,128)(2,1)S(1)} %pad_maximum_fusion.1.refs_0_, ...), custom_call_target="tpu_custom_call" | custom-call | flops 1610612736 | bytes 4194304 | tf_op jit(solution)/shard_map/pallas_call | solution.py:405
  60.9 6.3 %collective-permute-start.14 = (bf16[4,256,256]{2,1,0:T(8,128)(2,1)S(1)}, bf16[4,256,256]{2,1,0:T(8,128)(2,1)S(1)}, u32[]{:S(2)}, u32[]{:S(2)}) collective-permute-start(bf16[4,256,256]{2,1,0:T(8,128)(2,1)S(1)} %collective-permute-done.9.refs_0_), channel_id=1, source_target_pairs={{0,4},{1,5},{2,6},{3,7},{4,8},{5,9},{6,10},{7,11},{8,12},{9,13},{1... | collective-permute-start | bytes 1572872 | tf_op jit(solution)/shard_map/ppermute | solution.py:48
  67.2 2.1 %collective-permute-start.15 = (bf16[4,256,256]{2,1,0:T(8,128)(2,1)S(1)}, bf16[4,256,256]{2,1,0:T(8,128)(2,1)S(1)}, u32[]{:S(2)}, u32[]{:S(2)}) collective-permute-start(bf16[4,256,256]{2,1,0:T(8,128)(2,1)S(1)} %collective-permute-done.10.refs_1_), channel_id=1, source_target_pairs={{0,12},{1,13},{2,14},{3,15},{4,0},{5,1},{6,2},{7,3},{8,4},{9,5},{1... | collective-permute-start | bytes 1572872 | tf_op jit(solution)/shard_map/ppermute | solution.py:48
  69.3 12.0 %shard_map.78 = (f32[3,512,128]{2,1,0:T(8,128)S(1)}, f32[3,512,128]{2,1,0:T(8,128)S(1)}, f32[3,512,256]{2,1,0:T(8,128)S(1)}) custom-call(s32[296]{0:T(512)S(1)} %get-tuple-element.86.plan, bf16[4,512,256]{2,1,0:T(8,128)(2,1)S(1)} %pad_maximum_fusion.queries, ...), custom_call_target="tpu_custom_call", output_to_operand_aliasing={{0}: (4, {}), {1}: (5, {}), {2}: (6, {})} | custom-call | flops 1610612736 | bytes 4194304 | tf_op jit(solution)/shard_map/pallas_call | solution.py:405
  81.4 12.0 %shard_map.79 = (f32[3,512,128]{2,1,0:T(8,128)S(1)}, f32[3,512,128]{2,1,0:T(8,128)S(1)}, f32[3,512,256]{2,1,0:T(8,128)S(1)}) custom-call(s32[296]{0:T(512)S(1)} %get-tuple-element.86.plan, bf16[4,512,256]{2,1,0:T(8,128)(2,1)S(1)} %collective-permute-done.11.queries, ...), custom_call_target="tpu_custom_call", output_to_operand_aliasing={{0}: (4, {}), {1}: (5, {}), {2}: (6, {})} | custom-call | flops 1610612736 | bytes 4194304 | tf_op jit(solution)/shard_map/pallas_call | solution.py:405
  93.4 12.1 %shard_map.80 = (f32[3,512,128]{2,1,0:T(8,128)S(1)}, f32[3,512,128]{2,1,0:T(8,128)S(1)}, f32[3,512,256]{2,1,0:T(8,128)S(1)}) custom-call(s32[296]{0:T(512)S(1)} %get-tuple-element.86.plan, bf16[4,512,256]{2,1,0:T(8,128)(2,1)S(1)} %pad_maximum_fusion.queries, ...), custom_call_target="tpu_custom_call", output_to_operand_aliasing={{0}: (4, {}), {1}: (5, {}), {2}: (6, {})} | custom-call | flops 1610612736 | bytes 4194304 | tf_op jit(solution)/shard_map/pallas_call | solution.py:405
  105.5 12.0 %shard_map.81 = (f32[3,512,128]{2,1,0:T(8,128)S(1)}, f32[3,512,128]{2,1,0:T(8,128)S(1)}, f32[3,512,256]{2,1,0:T(8,128)S(1)}) custom-call(s32[296]{0:T(512)S(1)} %get-tuple-element.86.plan, bf16[4,512,256]{2,1,0:T(8,128)(2,1)S(1)} %collective-permute-done.11.queries, ...), custom_call_target="tpu_custom_call", output_to_operand_aliasing={{0}: (4, {}), {1}: (5, {}), {2}: (6, {})} | custom-call | flops 1610612736 | bytes 4194304 | tf_op jit(solution)/shard_map/pallas_call | solution.py:405
  117.5 10.0 %shard_map.83 = (bf16[3,528,256]{2,1,0:T(8,128)(2,1)S(1)}, f32[3,512,128]{2,1,0:T(8,128)S(1)}, f32[3,512,128]{2,1,0:T(8,128)S(1)}, f32[3,512,256]{2,1,0:T(8,128)S(1)}) custom-call(s32[296]{0:T(512)S(1)} %get-tuple-element.86.plan, ...), custom_call_target="tpu_custom_call", output_to_operand_aliasing={{1}: (4, {}), {2}: (5, {}), {3}: (6, {})} | custom-call | flops 1610612736 | bytes 4194304 | tf_op jit(solution)/shard_map/pallas_call | solution.py:405
  127.6 9.8 %shard_map.82 = (bf16[3,528,256]{2,1,0:T(8,128)(2,1)S(1)}, f32[3,512,128]{2,1,0:T(8,128)S(1)}, f32[3,512,128]{2,1,0:T(8,128)S(1)}, f32[3,512,256]{2,1,0:T(8,128)S(1)}) custom-call(s32[296]{0:T(512)S(1)} %get-tuple-element.86.plan, bf16[4,512,256]{2,1,0:T(8,128)(2,1)S(1)} %pad_maximum_fusion.queries, ...), custom_call_target="tpu_custom_call", output_to_operand_aliasing={{1}: (4, {}), {2}: (5, {}), {3}: (6, {})} | custom-call | flops 1610612736 | bytes 4194304 | tf_op jit(solution)/shard_map/pallas_call | solution.py:405
  138.0 3.5 %collective-permute-start.19 = (bf16[528,256]{1,0:T(8,128)(2,1)S(1)}, bf16[528,256]{1,0:T(8,128)(2,1)S(1)}, u32[]{:S(2)}, u32[]{:S(2)}) collective-permute-start(bf16[528,256]{1,0:T(8,128)(2,1)S(1)} %get-tuple-element.150), channel_id=1, source_target_pairs={{0,34},{1,3},{2,0},{3,33},{4,38},{5,7},{6,4},{7,37},{8,42},{9,11},... | collective-permute-start | bytes 811016 | tf_op jit(solution)/shard_map/ppermute | solution.py:48
  142.3 24.8 %shard_map.85 = (bf16[2,528,256]{2,1,0:T(8,128)(2,1)S(1)}, f32[2,512,128]{2,1,0:T(8,128)}, f32[2,512,128]{2,1,0:T(8,128)}, f32[2,512,256]{2,1,0:T(8,128)}) custom-call(s32[296]{0:T(512)S(1)} %get-tuple-element.86.plan, bf16[2,512,256]{2,1,0:T(8,128)(2,1)S(1)} %pad_maximum_fusion.3.queries, bf16[32,256,256]{2,1,0:T(8,128)(2,1)S(1)} %constant_dynamic-update-slice_fusion.refs_0_), custom_call_target="tpu_custom_call" | custom-call | flops 42949672 | bytes 41943 | tf_op jit(solution)/shard_map/pallas_call | solution.py:405
  167.1 1.4 collective-permute-start.17
  169.7 1.9 %shard_map.86 = bf16[64,4096]{1,0:T(8,128)(2,1)} custom-call(s32[5]{0:T(128)S(1)} %stack.41.place, bf16[528,256]{1,0:T(8,128)(2,1)S(1)} %get-tuple-element.164.mine, bf16[528,256]{1,0:T(8,128)(2,1)S(1)} %collective-permute-done.17.theirs, bf16[528,256]{1,0:T(8,128)(2,1)S(1)} %collective-permute-done.18.mate, ...), custom_call_target="tpu_custom_call" | custom-call | tf_op jit(solution)/shard_map/pallas_call | solution.py:536
  (63 shorter events, 12.9 us)
Async XLA Ops:
  0.1 0.8 copy-start.2
  2.4 15.7 %collective-permute-start.2 = (bf16[128,256]{1,0:T(8,128)(2,1)S(1)}, bf16[128,256]{1,0:T(8,128)(2,1)S(1)}, u32[]{:S(2)}, u32[]{:S(2)}) collective-permute-start(bf16[128,256]{1,0:T(8,128)(2,1)S(1)} %get-tuple-element.87), channel_id=1, source_target_pairs={{0,33},{1,32},{2,35},{3,34},{4,37},{5,36},{6,39},{7,38},{8,41},{9,... | collective-permute-start | bytes 196616 | tf_op jit(solution)/shard_map/ppermute | solution.py:48
  9.8 8.3 %collective-permute-start = (bf16[128,256]{1,0:T(8,128)(2,1)S(1)}, bf16[128,256]{1,0:T(8,128)(2,1)S(1)}, u32[]{:S(2)}, u32[]{:S(2)}) collective-permute-start(bf16[128,256]{1,0:T(8,128)(2,1)S(1)} %get-tuple-element.87), channel_id=1, source_target_pairs={{0,1},{1,0},{2,3},{3,2},{4,5},{5,4},{6,7},{7,6},{8,9},{9,8},{10,11... | collective-permute-start | bytes 196616 | tf_op jit(solution)/shard_map/ppermute | solution.py:48
  10.5 7.6 %collective-permute-start.1 = (bf16[128,256]{1,0:T(8,128)(2,1)S(1)}, bf16[128,256]{1,0:T(8,128)(2,1)S(1)}, u32[]{:S(2)}, u32[]{:S(2)}) collective-permute-start(bf16[128,256]{1,0:T(8,128)(2,1)S(1)} %get-tuple-element.84.own), channel_id=1, source_target_pairs={{0,32},{1,33},{2,34},{3,35},{4,36},{5,37},{6,38},{7,39},{8,40},{9,... | collective-permute-start | bytes 196616 | tf_op jit(solution)/shard_map/ppermute | solution.py:48
  11.1 1.0 copy-start
  18.4 9.4 %collective-permute-start.3 = (bf16[2,256,256]{2,1,0:T(8,128)(2,1)S(1)}, bf16[2,256,256]{2,1,0:T(8,128)(2,1)S(1)}, u32[]{:S(2)}, u32[]{:S(2)}) collective-permute-start(bf16[2,256,256]{2,1,0:T(8,128)(2,1)S(1)} %shard_map.75), channel_id=1, source_target_pairs={{0,64},{1,65},{2,66},{3,67},{4,68},{5,69},{6,70},{7,71},{8,72},{9,... | collective-permute-start | bytes 786440 | tf_op jit(solution)/shard_map/ppermute | solution.py:48
  19.8 9.1 %collective-permute-start.7 = (bf16[512,256]{1,0:T(8,128)(2,1)S(1)}, bf16[512,256]{1,0:T(8,128)(2,1)S(1)}, u32[]{:S(2)}, u32[]{:S(2)}) collective-permute-start(bf16[512,256]{1,0:T(8,128)(2,1)S(1)} %get-tuple-element.95), channel_id=1, source_target_pairs={{0,2},{1,35},{2,32},{3,1},{4,6},{5,39},{6,36},{7,5},{8,10},{9,43},... | collective-permute-start | bytes 786440 | tf_op jit(solution)/shard_map/ppermute | solution.py:48
  21.0 15.1 %collective-permute-start.8 = (bf16[512,256]{1,0:T(8,128)(2,1)S(1)}, bf16[512,256]{1,0:T(8,128)(2,1)S(1)}, u32[]{:S(2)}, u32[]{:S(2)}) collective-permute-start(bf16[512,256]{1,0:T(8,128)(2,1)S(1)} %get-tuple-element.96), channel_id=1, source_target_pairs={{0,35},{1,2},{2,1},{3,32},{4,39},{5,6},{6,5},{7,36},{8,43},{9,10},... | collective-permute-start | bytes 786440 | tf_op jit(solution)/shard_map/ppermute | solution.py:48
  24.5 11.7 %collective-permute-start.6 = (bf16[512,256]{1,0:T(8,128)(2,1)S(1)}, bf16[512,256]{1,0:T(8,128)(2,1)S(1)}, u32[]{:S(2)}, u32[]{:S(2)}) collective-permute-start(bf16[512,256]{1,0:T(8,128)(2,1)S(1)} %get-tuple-element.96), channel_id=1, source_target_pairs={{0,1},{1,0},{2,3},{3,2},{4,5},{5,4},{6,7},{7,6},{8,9},{9,8},{10,11... | collective-permute-start | bytes 786440 | tf_op jit(solution)/shard_map/ppermute | solution.py:48
  25.2 11.1 %collective-permute-start.5 = (bf16[2,256,256]{2,1,0:T(8,128)(2,1)S(1)}, bf16[2,256,256]{2,1,0:T(8,128)(2,1)S(1)}, u32[]{:S(2)}, u32[]{:S(2)}) collective-permute-start(bf16[2,256,256]{2,1,0:T(8,128)(2,1)S(1)} %shard_map.75), channel_id=1, source_target_pairs={{0,128},{1,129},{2,130},{3,131},{4,132},{5,133},{6,134},{7,135},{8... | collective-permute-start | bytes 786440 | tf_op jit(solution)/shard_map/ppermute | solution.py:48
  27.8 8.5 %collective-permute-start.4 = (bf16[2,256,256]{2,1,0:T(8,128)(2,1)S(1)}, bf16[2,256,256]{2,1,0:T(8,128)(2,1)S(1)}, u32[]{:S(2)}, u32[]{:S(2)}) collective-permute-start(bf16[2,256,256]{2,1,0:T(8,128)(2,1)S(1)} %shard_map.75), channel_id=1, source_target_pairs={{0,192},{1,193},{2,194},{3,195},{4,196},{5,197},{6,198},{7,199},{8... | collective-permute-start | bytes 786440 | tf_op jit(solution)/shard_map/ppermute | solution.py:48
  36.4 18.0 %collective-permute-start.11 = (bf16[4,512,256]{2,1,0:T(8,128)(2,1)S(1)}, bf16[4,512,256]{2,1,0:T(8,128)(2,1)S(1)}, u32[]{:S(2)}, u32[]{:S(2)}) collective-permute-start(bf16[4,512,256]{2,1,0:T(8,128)(2,1)S(1)} %pad_maximum_fusion.queries), channel_id=1, source_target_pairs={{0,16},{1,17},{2,18},{3,19},{4,20},{5,21},{6,22},{7,23},{8,24},{9,... | collective-permute-start | bytes 3145736 | tf_op jit(solution)/shard_map/ppermute | solution.py:48
  37.7 23.2 %collective-permute-start.9 = (bf16[4,256,256]{2,1,0:T(8,128)(2,1)S(1)}, bf16[4,256,256]{2,1,0:T(8,128)(2,1)S(1)}, u32[]{:S(2)}, u32[]{:S(2)}) collective-permute-start(bf16[4,256,256]{2,1,0:T(8,128)(2,1)S(1)} %pad_maximum_fusion.1.refs_0_), channel_id=1, source_target_pairs={{0,4},{1,5},{2,6},{3,7},{4,8},{5,9},{6,10},{7,11},{8,12},{9,13},{1... | collective-permute-start | bytes 1572872 | tf_op jit(solution)/shard_map/ppermute | solution.py:48
  39.4 21.5 %collective-permute-start.10 = (bf16[4,256,256]{2,1,0:T(8,128)(2,1)S(1)}, bf16[4,256,256]{2,1,0:T(8,128)(2,1)S(1)}, u32[]{:S(2)}, u32[]{:S(2)}) collective-permute-start(bf16[4,256,256]{2,1,0:T(8,128)(2,1)S(1)} %pad_maximum_fusion.2.refs_1_), channel_id=1, source_target_pairs={{0,12},{1,13},{2,14},{3,15},{4,0},{5,1},{6,2},{7,3},{8,4},{9,5},{1... | collective-permute-start | bytes 1572872 | tf_op jit(solution)/shard_map/ppermute | solution.py:48
  52.6 40.8 %collective-permute-start.13 = (bf16[4,256,256]{2,1,0:T(8,128)(2,1)S(1)}, bf16[4,256,256]{2,1,0:T(8,128)(2,1)S(1)}, u32[]{:S(2)}, u32[]{:S(2)}) collective-permute-start(bf16[4,256,256]{2,1,0:T(8,128)(2,1)S(1)} %pad_maximum_fusion.1.refs_0_), channel_id=1, source_target_pairs={{0,12},{1,13},{2,14},{3,15},{4,0},{5,1},{6,2},{7,3},{8,4},{9,5},{1... | collective-permute-start | bytes 1572872 | tf_op jit(solution)/shard_map/ppermute | solution.py:48
  54.2 39.2 %collective-permute-start.12 = (bf16[4,256,256]{2,1,0:T(8,128)(2,1)S(1)}, bf16[4,256,256]{2,1,0:T(8,128)(2,1)S(1)}, u32[]{:S(2)}, u32[]{:S(2)}) collective-permute-start(bf16[4,256,256]{2,1,0:T(8,128)(2,1)S(1)} %pad_maximum_fusion.2.refs_1_), channel_id=1, source_target_pairs={{0,4},{1,5},{2,6},{3,7},{4,8},{5,9},{6,10},{7,11},{8,12},{9,13},{1... | collective-permute-start | bytes 1572872 | tf_op jit(solution)/shard_map/ppermute | solution.py:48
  60.9 56.6 %collective-permute-start.14 = (bf16[4,256,256]{2,1,0:T(8,128)(2,1)S(1)}, bf16[4,256,256]{2,1,0:T(8,128)(2,1)S(1)}, u32[]{:S(2)}, u32[]{:S(2)}) collective-permute-start(bf16[4,256,256]{2,1,0:T(8,128)(2,1)S(1)} %collective-permute-done.9.refs_0_), channel_id=1, source_target_pairs={{0,4},{1,5},{2,6},{3,7},{4,8},{5,9},{6,10},{7,11},{8,12},{9,13},{1... | collective-permute-start | bytes 1572872 | tf_op jit(solution)/shard_map/ppermute | solution.py:48
  67.2 50.2 %collective-permute-start.15 = (bf16[4,256,256]{2,1,0:T(8,128)(2,1)S(1)}, bf16[4,256,256]{2,1,0:T(8,128)(2,1)S(1)}, u32[]{:S(2)}, u32[]{:S(2)}) collective-permute-start(bf16[4,256,256]{2,1,0:T(8,128)(2,1)S(1)} %collective-permute-done.10.refs_1_), channel_id=1, source_target_pairs={{0,12},{1,13},{2,14},{3,15},{4,0},{5,1},{6,2},{7,3},{8,4},{9,5},{1... | collective-permute-start | bytes 1572872 | tf_op jit(solution)/shard_map/ppermute | solution.py:48
  127.5 9.9 %collective-permute-start.16 = (bf16[3,528,256]{2,1,0:T(8,128)(2,1)S(1)}, bf16[3,528,256]{2,1,0:T(8,128)(2,1)S(1)}, u32[]{:S(2)}, u32[]{:S(2)}) collective-permute-start(bf16[3,528,256]{2,1,0:T(8,128)(2,1)S(1)} %get-tuple-element.148), channel_id=1, source_target_pairs={{0,16},{1,17},{2,18},{3,19},{4,20},{5,21},{6,22},{7,23},{8,24},{9,... | collective-permute-start | bytes 2433032 | tf_op jit(solution)/shard_map/ppermute | solution.py:48
  137.9 30.6 %collective-permute-start.18 = (bf16[528,256]{1,0:T(8,128)(2,1)S(1)}, bf16[528,256]{1,0:T(8,128)(2,1)S(1)}, u32[]{:S(2)}, u32[]{:S(2)}) collective-permute-start(bf16[528,256]{1,0:T(8,128)(2,1)S(1)} %get-tuple-element.149), channel_id=1, source_target_pairs={{0,1},{1,0},{2,3},{3,2},{4,5},{5,4},{6,7},{7,6},{8,9},{9,8},{10,11... | collective-permute-start | bytes 811016 | tf_op jit(solution)/shard_map/ppermute | solution.py:48
  138.0 30.5 %collective-permute-start.19 = (bf16[528,256]{1,0:T(8,128)(2,1)S(1)}, bf16[528,256]{1,0:T(8,128)(2,1)S(1)}, u32[]{:S(2)}, u32[]{:S(2)}) collective-permute-start(bf16[528,256]{1,0:T(8,128)(2,1)S(1)} %get-tuple-element.150), channel_id=1, source_target_pairs={{0,34},{1,3},{2,0},{3,33},{4,38},{5,7},{6,4},{7,37},{8,42},{9,11},... | collective-permute-start | bytes 811016 | tf_op jit(solution)/shard_map/ppermute | solution.py:48
  141.5 27.0 %collective-permute-start.20 = (bf16[528,256]{1,0:T(8,128)(2,1)S(1)}, bf16[528,256]{1,0:T(8,128)(2,1)S(1)}, u32[]{:S(2)}, u32[]{:S(2)}) collective-permute-start(bf16[528,256]{1,0:T(8,128)(2,1)S(1)} %get-tuple-element.151), channel_id=1, source_target_pairs={{0,35},{1,2},{2,1},{3,32},{4,39},{5,6},{6,5},{7,36},{8,43},{9,10},... | collective-permute-start | bytes 811016 | tf_op jit(solution)/shard_map/ppermute | solution.py:48
  142.2 27.5 %copy-start.1 = (bf16[64,4096]{1,0:T(8,128)(2,1)S(1)}, bf16[64,4096]{1,0:T(8,128)(2,1)}, u32[]{:S(2)}) copy-start(bf16[64,4096]{1,0:T(8,128)(2,1)} %gate.1) | copy-start | bytes 1572868
  167.1 2.6 %collective-permute-start.17 = (bf16[528,256]{1,0:T(8,128)(2,1)S(1)}, bf16[528,256]{1,0:T(8,128)(2,1)S(1)}, u32[]{:S(2)}, u32[]{:S(2)}) collective-permute-start(bf16[528,256]{1,0:T(8,128)(2,1)S(1)} %get-tuple-element.163), channel_id=1, source_target_pairs={{0,16},{1,17},{2,18},{3,19},{4,20},{5,21},{6,22},{7,23},{8,24},{9,... | collective-permute-start | bytes 811016 | tf_op jit(solution)/shard_map/ppermute | solution.py:48
  (4 other events, 2.9 us)
